TPU v7x, 32 devices: a whole 2x2x4 slice. The times are simulated.
32 devices in a mesh: grp: 2 (over y), seq: 4 (over z), head: 2 (over x), clip: 2 (over core).
Axes of the slice: x: 2, y: 2, z: 4, core: 2. Of those that a mesh axis runs over, the one named last changes fastest.
Arguments:
- query_states: bfloat16 [4, 2048, 1536], P(('grp', 'clip'), 'seq', 'head'), parts along dimension 0, may hold values from -64 to 64
- key_states: bfloat16 [4, 2048, 1536], P(('grp', 'clip'), 'seq', 'head'), parts along dimension 0, may hold values from -4 to 4
- value_states: bfloat16 [4, 2048, 1536], P(('grp', 'clip'), 'seq', 'head'), parts along dimension 0, may hold values from -5 to 5
- output_grad: bfloat16 [4, 2048, 3072], P(('grp', 'clip'), 'seq', 'head'), parts along dimension 0, may hold values from -48 to 48
- w_out: bfloat16 [1536, 3072], P('head'), may hold values from -0.15625 to 0.15625
- key_list: int32 [4, 8, 8], P(('grp', 'clip')), parts along dimension 0, may hold values from 0 to 7, as said below
- key_count: int32 [4, 8], P(('grp', 'clip')), parts along dimension 0, may hold values from 1 to 8, as said below
Outputs:
- query_grad: bfloat16 [4, 2048, 1536], P(('grp', 'clip'), 'seq', 'head'), parts along dimension 0
- key_grad: bfloat16 [4, 2048, 1536], P(('grp', 'clip'), 'seq', 'head'), parts along dimension 0
- value_grad: bfloat16 [4, 2048, 1536], P(('grp', 'clip'), 'seq', 'head'), parts along dimension 0
- grad_features: float32 [4, 12, 3], P(('grp', 'clip'), 'head'), parts along dimension 0
There are 2 independent parts, one for each index of `grp`. A program takes and returns all parts, laid end to end along the dimension named above; an argument that names none is the same for every part. Nothing has to cross between parts.
Inputs may be any that keep to these rules, and one draw needn't show every extreme that they name: Tile i lies in frame block i // 4 at place i % 4. For each clip and query tile i the first key_count entries of key_list are distinct key tiles in ascending order, among them i itself, each at a place within 2 of i's place, in i's frame block or in the other one; the remaining entries equal i. `key_count`: in every draw some query tile lists 8 key tiles.
All inputs are finite; a program needn't handle non-finite values.
Results may differ from a plain program's by a relative error of at most 0.035.
Values may be sent and summed in bfloat16 or wider, within the bound.
A program may use at most 128 MiB of HBM per device.

v0:
```python
import jax
import jax.numpy as jnp
from jax import lax
from jax.sharding import PartitionSpec as P

HD = 128
TILE = 256


def attend(query_tiles, key_buf, value_buf, grad_tiles, buf_slots, counts):
    score_scale = HD ** (-0.5)
    tile_count, tile_rows, feat_width = query_tiles.shape
    slot_count = buf_slots.shape[1]
    key_span = slot_count * tile_rows
    buf_tiles = key_buf.shape[0]
    key_sel = key_buf[buf_slots].reshape(tile_count, key_span, feat_width)
    value_sel = value_buf[buf_slots].reshape(tile_count, key_span, feat_width)
    allowed = jnp.arange(key_span)[None, :] // tile_rows < counts[:, None]

    def head_step(head_idx, carried):
        query_acc, key_acc, value_acc = carried
        col_start = head_idx * HD
        query_head = lax.dynamic_slice_in_dim(query_tiles, col_start, HD, 2)
        key_head = lax.dynamic_slice_in_dim(key_sel, col_start, HD, 2)
        value_head = lax.dynamic_slice_in_dim(value_sel, col_start, HD, 2)
        grad_head = lax.dynamic_slice_in_dim(grad_tiles, col_start, HD, 2)
        scores = (
            jnp.einsum("iqe,ike->iqk", query_head, key_head, preferred_element_type=jnp.float32)
            * score_scale
        )
        scores = jnp.where(allowed[:, None, :], scores, -jnp.inf)
        row_max = jnp.max(scores, axis=-1, keepdims=True)
        log_norm = row_max + jnp.log(jnp.sum(jnp.exp(scores - row_max), axis=-1, keepdims=True))
        weights = jnp.exp(scores - log_norm)
        weights_b = weights.astype(jnp.bfloat16)
        attn_out = jnp.einsum(
            "iqk,ike->iqe", weights_b, value_head, preferred_element_type=jnp.float32
        ).astype(jnp.bfloat16)
        row_delta = jnp.sum(
            grad_head.astype(jnp.float32) * attn_out.astype(jnp.float32), axis=-1, keepdims=True
        )
        dprob = jnp.einsum(
            "iqe,ike->iqk", grad_head, value_head, preferred_element_type=jnp.float32
        )
        dscore = (weights * (dprob - row_delta)).astype(jnp.bfloat16)
        query_head_grad = score_scale * jnp.einsum(
            "iqk,ike->iqe", dscore, key_head, preferred_element_type=jnp.float32
        )
        key_head_grad = score_scale * jnp.einsum(
            "iqk,iqe->ike", dscore, query_head, preferred_element_type=jnp.float32
        )
        value_head_grad = jnp.einsum(
            "iqk,iqe->ike", weights_b, grad_head, preferred_element_type=jnp.float32
        )
        query_acc = lax.dynamic_update_slice_in_dim(query_acc, query_head_grad, col_start, 2)
        key_acc = lax.dynamic_update_slice_in_dim(key_acc, key_head_grad, col_start, 2)
        value_acc = lax.dynamic_update_slice_in_dim(value_acc, value_head_grad, col_start, 2)
        return (query_acc, key_acc, value_acc)

    start_state = (
        jnp.zeros((tile_count, tile_rows, feat_width), jnp.float32),
        jnp.zeros((tile_count, key_span, feat_width), jnp.float32),
        jnp.zeros((tile_count, key_span, feat_width), jnp.float32),
    )
    query_full, key_sel_grad, value_sel_grad = lax.fori_loop(
        0, feat_width // HD, head_step, start_state
    )
    live_slot = jnp.arange(slot_count)[None, :] < counts[:, None]
    routing = (
        (buf_slots[:, :, None] == jnp.arange(buf_tiles)[None, None, :]) & live_slot[:, :, None]
    ).astype(jnp.float32)
    key_grad_buf = jnp.einsum(
        "imb,imr->br",
        routing,
        key_sel_grad.reshape(tile_count, slot_count, tile_rows * feat_width),
        precision=lax.Precision.HIGHEST,
    )
    value_grad_buf = jnp.einsum(
        "imb,imr->br",
        routing,
        value_sel_grad.reshape(tile_count, slot_count, tile_rows * feat_width),
        precision=lax.Precision.HIGHEST,
    )
    return (
        query_full,
        key_grad_buf.reshape(buf_tiles, tile_rows, feat_width),
        value_grad_buf.reshape(buf_tiles, tile_rows, feat_width),
    )


def head_squares(grads_full, head_count):
    rows = grads_full.reshape(-1, head_count, HD)
    return jnp.sum(rows * rows, axis=(0, 2))


def per_device(query_states, key_states, value_states, output_grad, w_out, key_list, key_count):
    seq_count = lax.axis_size("seq")
    seq_index = lax.axis_index("seq")
    tok_rows = query_states.shape[1]
    feat_width = query_states.shape[2]
    head_count = feat_width // HD
    tile_count = tok_rows // TILE
    first_tile = seq_index * tile_count
    own_lists = lax.dynamic_slice_in_dim(key_list[0], first_tile, tile_count, 0)
    own_counts = lax.dynamic_slice_in_dim(key_count[0], first_tile, tile_count, 0)
    grad_out = lax.dot_general(
        lax.all_gather(output_grad, "head", axis=2, tiled=True)[0],
        w_out,
        (((1,), (1,)), ((), ())),
        preferred_element_type=jnp.float32,
    ).astype(jnp.bfloat16)
    query_tiles = query_states[0].reshape(tile_count, TILE, feat_width)
    grad_tiles = grad_out.reshape(tile_count, TILE, feat_width)
    key_whole, value_whole = (
        lax.all_gather(key_states, "seq", axis=1, tiled=True),
        lax.all_gather(value_states, "seq", axis=1, tiled=True),
    )
    key_buf = key_whole[0].reshape(-1, TILE, feat_width)
    value_buf = value_whole[0].reshape(-1, TILE, feat_width)
    query_full, key_grad_buf, value_grad_buf = attend(
        query_tiles, key_buf, value_buf, grad_tiles, own_lists, own_counts
    )
    buf_rows = key_grad_buf.shape[0] * TILE
    key_sum, value_sum = (
        lax.psum_scatter(
            key_grad_buf.reshape(1, buf_rows, feat_width).astype(jnp.bfloat16),
            "seq",
            scatter_dimension=1,
            tiled=True,
        ).astype(jnp.float32),
        lax.psum_scatter(
            value_grad_buf.reshape(1, buf_rows, feat_width).astype(jnp.bfloat16),
            "seq",
            scatter_dimension=1,
            tiled=True,
        ).astype(jnp.float32),
    )
    key_full = key_sum[0]
    value_full = value_sum[0]
    query_rows = query_full.reshape(tok_rows, feat_width)
    local_sums = jnp.stack(
        [
            head_squares(query_rows, head_count),
            head_squares(key_full, head_count),
            head_squares(value_full, head_count),
        ],
        axis=-1,
    )
    total_sums = lax.psum(local_sums, "seq")
    grad_features = jnp.log(total_sums / (seq_count * tok_rows * HD) + 1e-06)
    return (
        query_rows.astype(jnp.bfloat16)[None],
        key_full.astype(jnp.bfloat16)[None],
        value_full.astype(jnp.bfloat16)[None],
        grad_features[None],
    )


def solution(mesh):
    in_specs = (
        P(("grp", "clip"), "seq", "head"),
        P(("grp", "clip"), "seq", "head"),
        P(("grp", "clip"), "seq", "head"),
        P(("grp", "clip"), "seq", "head"),
        P("head", None),
        P(("grp", "clip"), None, None),
        P(("grp", "clip"), None),
    )
    out_specs = (
        P(("grp", "clip"), "seq", "head"),
        P(("grp", "clip"), "seq", "head"),
        P(("grp", "clip"), "seq", "head"),
        P(("grp", "clip"), "head", None),
    )
    return jax.shard_map(
        per_device, mesh=mesh, in_specs=in_specs, out_specs=out_specs, check_vma=False
    )
```

profile of v0, /device:TPU:0, one launch (start us, length us, event | category | flops | bytes accessed | tf_op | source)
XLA Modules:
  0.0 461.2 jit_solution(8411246772068753391)
XLA Ops:
  11.1 46.2 %all-gather.6.cloned.1.call-done = bf16[1,512,3072]{2,1,0:T(8,128)(2,1)} async-done(((bf16[1,512,1536]{2,1,0:T(8,128)(2,1)}), bf16[1,512,3072]{2,1,0:T(8,128)(2,1)}) %all-gather.6.cloned.1.call-update) | async-done | bytes 3145744 | tf_op jit(solution)/shard_map/all_gather | solution.py:107
  57.3 5.9 %fusion.28 = bf16[512,768]{1,0:T(8,128)(2,1)S(1)} fusion(bf16[768,3072]{1,0:T(8,128)(2,1)} %param.13, bf16[1,512,3072]{2,1,0:T(8,128)(2,1)} %all-gather.6.cloned.1.call-done), kind=kOutput, calls=%fused_computation.42 | convolution fusion | flops 2416312320 | bytes 8650752 | tf_op jit(solution)/shard_map/dot_general | solution.py:106
  63.2 59.2 %all-gather.4.cloned.1.call-done = bf16[1,2048,768]{2,1,0:T(8,128)(2,1)} async-done(((bf16[1,512,768]{2,1,0:T(8,128)(2,1)}), bf16[1,2048,768]{2,1,0:T(8,128)(2,1)}) %all-gather.4.cloned.1.call-update) | async-done | bytes 3145744 | tf_op jit(solution)/shard_map/all_gather | solution.py:115
  122.4 5.6 %gather_fusion = bf16[16,256,768]{2,1,0:T(8,128)(2,1)} fusion(bf16[8,256,768]{2,1,0:T(8,128)(2,1)} %bitcast.50, s32[1024]{0:T(1024)S(1)} %pad_clamp_fusion), kind=kCustom, calls=%fused_computation | custom fusion | bytes 12582976 | tf_op jit(solution)/shard_map/gather | solution.py:16
  127.9 58.2 %all-gather.8.cloned.1.call-done = bf16[1,2048,768]{2,1,0:T(8,128)(2,1)} async-done(((bf16[1,512,768]{2,1,0:T(8,128)(2,1)}), bf16[1,2048,768]{2,1,0:T(8,128)(2,1)}) %all-gather.8.cloned.1.call-update) | async-done | bytes 3145744 | tf_op jit(solution)/shard_map/all_gather | solution.py:116
  186.1 5.5 %gather_fusion.1 = bf16[16,256,768]{2,1,0:T(8,128)(2,1)} fusion(bf16[8,256,768]{2,1,0:T(8,128)(2,1)} %bitcast.51, s32[1024]{0:T(1024)S(1)} %pad_clamp_fusion), kind=kCustom, calls=%fused_computation.1 | custom fusion | bytes 12582976 | tf_op jit(solution)/shard_map/gather | solution.py:17
  191.7 5.4 %broadcast.103 = f32[2,2048,768]{2,1,0:T(8,128)} broadcast(f32[]{:T(128)} %constant.78.clone.1), dimensions={} | broadcast | bytes 12582916 | tf_op jit(solution)/shard_map/broadcast.13
  197.0 5.3 %broadcast.103.clone = f32[2,2048,768]{2,1,0:T(8,128)} broadcast(f32[]{:T(128)} %constant.78.clone.1), dimensions={} | broadcast | bytes 12582916 | tf_op jit(solution)/shard_map/broadcast.13
  202.4 92.5 %while.18 = (s32[]{:T(128)}, f32[2,256,768]{2,1,0:T(8,128)S(1)}, f32[2,2048,768]{2,1,0:T(8,128)}, f32[2,2048,768]{2,1,0:T(8,128)}, bf16[2,256,768]{2,1,0:T(8,128...) while((s32[]{:T(128)}, f32[2,256,768]{2,1,0:T(8,128)S(1)}, ...), condition=%wide.region_4.5_spmd.clone, body=%wide.region_0.4_spmd.clone.sunk | while | flops 1625164800 | bytes 36614328 | solution.py:65
  205.6 2.6 convolution_dynamic-update-slice_fusion.2
  212.6 3.4 fusion.74
  220.9 2.6 convolution_dynamic-update-slice_fusion.2
  225.7 2.3 multiply_convert_fusion.2
  228.0 3.3 fusion.74
  236.2 2.7 convolution_dynamic-update-slice_fusion.2
  243.4 3.3 fusion.74
  251.6 2.8 convolution_dynamic-update-slice_fusion.2
  258.8 3.4 fusion.74
  267.1 2.7 convolution_dynamic-update-slice_fusion.2
  274.2 3.4 fusion.74
  282.5 2.6 convolution_dynamic-update-slice_fusion.2
  287.3 2.3 multiply_convert_fusion.2
  289.6 3.4 fusion.74
  296.1 13.2 %reshape.176 = f32[2,8,196608]{2,1,0:T(8,128)} reshape(f32[2,2048,768]{2,1,0:T(8,128)} %get-tuple-element.161) | data formatting | bytes 25165824 | tf_op jit(solution)/shard_map/reshape | solution.py:75
  309.3 7.6 %fusion.24 = bf16[8,196608]{1,0:T(8,128)(2,1)S(1)} fusion(f32[2,8,196608]{2,1,0:T(8,128)} %reshape.176, s32[2,8]{1,0:T(2,128)S(1)} %dynamic-slice_bitcast_fusion, pred[2,8]{1,0:T(4,128)(4,1)S(1)} %iota_compare_fusion.1), kind=kOutput, calls=%fused_computation.35 | convolution fusion | flops 303563008 | bytes 15728720 | tf_op jit(solution)/shard_map/imb,imr->br/dot_general | solution.py:72
  316.9 3.2 convert_element_type.94
  320.1 13.3 %reshape.177 = f32[2,8,196608]{2,1,0:T(8,128)} reshape(f32[2,2048,768]{2,1,0:T(8,128)} %get-tuple-element.162) | data formatting | bytes 25165824 | tf_op jit(solution)/shard_map/reshape | solution.py:81
  333.5 7.6 %fusion.25 = bf16[8,196608]{1,0:T(8,128)(2,1)S(1)} fusion(f32[2,8,196608]{2,1,0:T(8,128)} %reshape.177, s32[2,8]{1,0:T(2,128)S(1)} %dynamic-slice_bitcast_fusion, pred[2,8]{1,0:T(4,128)(4,1)S(1)} %iota_compare_fusion.1), kind=kOutput, calls=%fused_computation.36 | convolution fusion | flops 303563008 | bytes 15728720 | tf_op jit(solution)/shard_map/imb,imr->br/dot_general | solution.py:78
  341.1 3.1 convert_element_type.96
  346.7 32.4 %reduce-scatter.3.cloned.1.call-done = bf16[1,512,768]{2,1,0:T(8,128)(2,1)} async-done(((bf16[1,2048,768]{2,1,0:T(8,128)(2,1)}), bf16[1,512,768]{2,1,0:T(8,128)(2,1)}) %reduce-scatter.3.cloned.1.call-update) | async-done | bytes 786448 | tf_op jit(solution)/shard_map/reduce_scatter | solution.py:125
  380.6 61.6 %reduce-scatter.5.cloned.1.call-done = bf16[1,512,768]{2,1,0:T(8,128)(2,1)} async-done(((bf16[1,2048,768]{2,1,0:T(8,128)(2,1)}), bf16[1,512,768]{2,1,0:T(8,128)(2,1)}) %reduce-scatter.5.cloned.1.call-update) | async-done | bytes 786448 | tf_op jit(solution)/shard_map/reduce_scatter | solution.py:131
  443.6 10.4 %psum.7 = f32[6,3]{0,1:T(4,128)S(1)} all-reduce(f32[6,3]{0,1:T(4,128)S(1)} %pad_maximum_fusion), channel_id=1, replica_groups=mesh['grp'=2,'seq'=4,'head'=2,'clip'=2] {'seq'}, use_global_device_ids=true, to_apply=%region_13.14 | all-reduce | flops 18 | bytes 144 | tf_op jit(solution)/shard_map/psum | solution.py:149
  (75 shorter events, 62.4 us)
Async XLA Ops:
  7.2 3.1 copy-start
  7.2 50.1 %all-gather.6.cloned.1.call-start = ((), (), s32[]{:S(2)}) async-start(), calls=%async_computation.3 | async-start | bytes 4718592 | tf_op jit(solution)/shard_map/all_gather | solution.py:107
  7.9 114.4 %all-gather.4.cloned.1.call-start = ((), (), s32[]{:S(2)}) async-start(), calls=%async_computation.2 | async-start | bytes 3932160 | tf_op jit(solution)/shard_map/all_gather | solution.py:115
  8.7 177.5 %all-gather.8.cloned.1.call-start = ((), (), s32[]{:S(2)}) async-start(), calls=%async_computation.4 | async-start | bytes 3932160 | tf_op jit(solution)/shard_map/all_gather | solution.py:116
  9.4 369.8 %reduce-scatter.3.cloned.1.call-start = ((), (), s32[]{:S(2)}) async-start(), calls=%async_computation.5 | async-start | bytes 3932160 | tf_op jit(solution)/shard_map/reduce_scatter | solution.py:125
  294.9 1.1 copy-start.2
  320.1 122.1 %reduce-scatter.5.cloned.1.call-start = ((), (), s32[]{:S(2)}) async-start(), calls=%async_computation.6 | async-start | bytes 3932160 | tf_op jit(solution)/shard_map/reduce_scatter | solution.py:131
  341.1 113.6 %copy-start.1 = (s32[1,8]{1,0:T(1,128)S(1)}, s32[1,8]{1,0:T(1,128)}, u32[]{:S(2)}) copy-start(s32[1,8]{1,0:T(1,128)} %param.15) | copy-start | bytes 100
  344.2 1.4 copy-start.3
Sparse Core Ops, SparseCore 0:
  9.6 47.6 all-gather.5
  58.8 63.4 all-gather.3
  123.9 62.1 all-gather.7
  320.2 58.8 reduce-scatter.2
  381.9 60.2 reduce-scatter.4
where the time goes:
time: 463 us; the launch traced here: 461 us
  waiting for transfers between devices  260 us (56%)
  matrix products  108 us (23%)
  local copies, waits for them, and re-layouts  58.6 us (13%)
  between operations  13.9 us (3%)
  blocking collectives  10.4 us (2%)
  other arithmetic  9.63 us (2%)
    reduce_scatter x1, waiting for transfers between devices, per_device(): lax.psum_scatter(value_grad_buf.reshape(1, buf_rows, feat_width).astype(j...  61.6 us
    all_gather x1, waiting for transfers between devices, per_device(): lax.all_gather(key_states, 'seq', axis=1, tiled=True)  59.2 us
    all_gather x1, waiting for transfers between devices, per_device(): lax.all_gather(value_states, 'seq', axis=1, tiled=True)  58.2 us
    all_gather x1, waiting for transfers between devices, per_device(): lax.all_gather(output_grad, 'head', axis=2, tiled=True)[0]  46.2 us
    reduce_scatter x1, waiting for transfers between devices, per_device(): lax.psum_scatter(key_grad_buf.reshape(1, buf_rows, feat_width).astype(jnp...  32.4 us
    dot_general x6, matrix products, head_step(): jnp.einsum('iqk,iqe->ike', dscore, query_head, preferred_element_type=jnp...  20.2 us
    dot_general x6, matrix products, head_step(): jnp.einsum('iqk,iqe->ike', weights_b, grad_head, preferred_element_type=j...  16 us
    dot_general x6, matrix products, head_step(): jnp.einsum('iqe,ike->iqk', grad_head, value_head, preferred_element_type=...  13.7 us
  transfers between devices with their start and end apart: 5, of which 5 were waited for; matrix products, arithmetic and copies ran while one was open for 9% of the time, Pallas kernels for 0%

commit v1 on v0

--- a/solution.py
+++ b/solution.py
@@ -1,6 +1,11 @@
+import functools
+import math
+
 import jax
 import jax.numpy as jnp
 from jax import lax
+from jax.experimental import pallas as pl
+from jax.experimental.pallas import tpu as pltpu
 from jax.sharding import PartitionSpec as P
 
 HD = 128
@@ -93,7 +98,7 @@
     return jnp.sum(rows * rows, axis=(0, 2))
 
 
-def per_device(query_states, key_states, value_states, output_grad, w_out, key_list, key_count):
+def gathered_plan(query_states, key_states, value_states, output_grad, w_out, key_list, key_count):
     seq_count = lax.axis_size("seq")
     seq_index = lax.axis_index("seq")
     tok_rows = query_states.shape[1]
@@ -156,6 +161,392 @@
     )
 
 
+MESH_ID = pl.DeviceIdType.MESH
+VMEM_BYTES = 58 * 1024 * 1024
+NEG_BIG = -1e30
+F32 = jnp.float32
+BF16 = jnp.bfloat16
+
+
+def dot_nt(a, b):
+    return lax.dot_general(a, b, (((1,), (1,)), ((), ())), preferred_element_type=F32)
+
+
+def dot_nn(a, b):
+    return lax.dot_general(a, b, (((1,), (0,)), ((), ())), preferred_element_type=F32)
+
+
+def fused_kernel(
+    n, nh, q_ref, k_ref, v_ref, og_ref, w_ref, bias_ref,
+    dq_ref, dk_ref, dv_ref, feat_ref,
+    q_all, g_all, og_all, g_acc, stat_all, comb, part, chain, kt_ref, acc_k, acc_v, acc_q, sq_all,
+    og_send, og_recv, q_send, q_recv, g_send, g_recv, stat_send, stat_recv,
+    chain_send, chain_recv, sq_send, sq_recv,
+):
+    z = lax.axis_index("seq")
+    hx = lax.axis_index("head")
+    rows, width = q_ref.shape
+    heads = width // HD
+    feats = og_ref.shape[1]
+    key_tiles = rows // TILE
+    scale = HD ** (-0.5)
+    scale2 = scale * math.log2(math.e)
+    has_left = z > 0
+    has_right = z < n - 1
+
+    def remote(src, dst, ssem, rsem, axis, idx):
+        return pltpu.make_async_remote_copy(
+            src_ref=src, dst_ref=dst, send_sem=ssem, recv_sem=rsem,
+            device_id={axis: idx}, device_id_type=MESH_ID,
+        )
+
+    def cols(h):
+        return pl.ds(pl.multiple_of(h * HD, HD), HD)
+
+    barrier = pltpu.get_barrier_semaphore()
+    for i in range(1, n):
+        pl.semaphore_signal(barrier, inc=1, device_id={"seq": lax.rem(z + i, n)}, device_id_type=MESH_ID)
+    for i in range(1, nh):
+        pl.semaphore_signal(barrier, inc=1, device_id={"head": lax.rem(hx + i, nh)}, device_id_type=MESH_ID)
+    pl.semaphore_wait(barrier, n - 1 + nh - 1)
+
+    def og_copy(i):
+        return remote(og_ref, og_all.at[hx], og_send.at[i], og_recv.at[hx], "head", lax.rem(hx + i, nh))
+
+    def og_arrival(j):
+        return remote(og_all.at[j], og_all.at[j], og_send.at[0], og_recv.at[j], "head", hx)
+
+    def q_copy(b, way):
+        return remote(q_all.at[b], q_all.at[b], q_send.at[way, b], q_recv.at[b], "seq", z + (1 - 2 * way))
+
+    def g_copy(b, h, way):
+        return remote(g_all.at[b, h], g_all.at[b, h], g_send.at[way, b, h], g_recv.at[b, h], "seq", z + (1 - 2 * way))
+
+    def stat_copy(h, i):
+        return remote(stat_all.at[z, h], stat_all.at[z, h], stat_send.at[h, i], stat_recv.at[z, h], "seq", lax.rem(z + i, n))
+
+    def stat_arrival(d, h):
+        return remote(stat_all.at[d, h], stat_all.at[d, h], stat_send.at[h, 0], stat_recv.at[d, h], "seq", z)
+
+    def chain_copy(b, h, way):
+        slot = b if way == 0 else jnp.where(b == z - 1, n, b)
+        return remote(part.at[b, h], chain.at[slot, h], chain_send.at[b, h], chain_recv.at[slot, h], "seq", z + (1 - 2 * way))
+
+    def chain_arrival(slot, h):
+        return remote(chain.at[slot, h], chain.at[slot, h], chain_send.at[0, h], chain_recv.at[slot, h], "seq", z)
+
+    def sq_copy(i):
+        return remote(sq_all.at[z], sq_all.at[z], sq_send.at[i], sq_recv.at[z], "seq", lax.rem(z + i, n))
+
+    def sq_arrival(d):
+        return remote(sq_all.at[d], sq_all.at[d], sq_send.at[0], sq_recv.at[d], "seq", z)
+
+    def both_ways(copy_of):
+        @pl.when(has_right)
+        def _():
+            copy_of(0)
+
+        @pl.when(has_left)
+        def _():
+            copy_of(1)
+
+    for i in range(1, nh):
+        og_copy(i).start()
+    q_all[z] = q_ref[...]
+    both_ways(lambda way: q_copy(z, way).start())
+
+    wide = 256 if width % 256 == 0 else HD
+
+    def features_of(block, j, add):
+        span = pl.ds(pl.multiple_of(j * feats, HD), feats)
+
+        @pl.loop(0, width // wide)
+        def _(c):
+            at = pl.ds(pl.multiple_of(c * wide, wide), wide)
+            term = dot_nt(block[...], w_ref[at, span])
+            if add:
+                g_acc[c] = g_acc[c] + term
+            else:
+                g_acc[c] = term
+
+    features_of(og_ref, hx, False)
+
+    def q_hop(s):
+        @pl.when(z - s >= 0)
+        def _():
+            q_copy(z - s, 0).wait_recv()
+
+            @pl.when(has_right)
+            def _():
+                q_copy(z - s, 0).start()
+
+        @pl.when(z + s < n)
+        def _():
+            q_copy(z + s, 1).wait_recv()
+
+            @pl.when(has_left)
+            def _():
+                q_copy(z + s, 1).start()
+
+    early = min(2, n - 1)
+    for s in range(1, early + 1):
+        q_hop(s)
+    for i in range(1, nh):
+        j = lax.rem(hx + i, nh)
+        og_arrival(j).wait_recv()
+        features_of(og_all.at[j], j, True)
+    for h in range(heads):
+        lo = h * HD
+        g_all[z, h] = g_acc[lo // wide, :, lo % wide : lo % wide + HD].astype(BF16)
+        both_ways(lambda way: g_copy(z, h, way).start())
+    for s in range(early + 1, n):
+        q_hop(s)
+
+    def g_hop(s, h):
+        @pl.when((h >= 0) & (h < heads))
+        def _():
+            @pl.when(z - s >= 0)
+            def _():
+                g_copy(z - s, h, 0).wait_recv()
+                if s < n - 1:
+                    @pl.when(has_right)
+                    def _():
+                        g_copy(z - s, h, 0).start()
+
+            @pl.when(z + s < n)
+            def _():
+                g_copy(z + s, h, 1).wait_recv()
+                if s < n - 1:
+                    @pl.when(has_left)
+                    def _():
+                        g_copy(z + s, h, 1).start()
+
+    def logits(b, h, j):
+        t = dot_nt(k_ref[j * TILE : (j + 1) * TILE, cols(h)], q_all[b, :, cols(h)])
+        return t * scale2 + bias_ref[b, j : j + 1, :]
+
+    def dprobs(b, h, j):
+        return dot_nt(v_ref[j * TILE : (j + 1) * TILE, cols(h)], g_all[b, h])
+
+    def first_pass(h):
+        @pl.loop(0, n)
+        def _(b):
+            ts = [logits(b, h, j) for j in range(key_tiles)]
+            top = functools.reduce(jnp.maximum, [jnp.max(t, axis=0, keepdims=True) for t in ts])
+            total = jnp.zeros((1, rows), F32)
+            eps = jnp.zeros((1, rows), F32)
+            for j in range(key_tiles):
+                p = jnp.exp2(ts[j] - top)
+                total += jnp.sum(p, axis=0, keepdims=True)
+                eps += jnp.sum(p * dprobs(b, h, j), axis=0, keepdims=True)
+            stat_all[z, h, b, 0:1, :] = top + jnp.log2(total)
+            stat_all[z, h, b, 1:2, :] = eps / total
+
+        for i in range(1, n):
+            stat_copy(h, i).start()
+
+    def second_pass(h):
+        for i in range(1, n):
+            stat_arrival(lax.rem(z + i, n), h).wait_recv()
+        for b in range(n):
+            logs = [stat_all[d, h, b, 0:1, :] for d in range(n)]
+            top = functools.reduce(jnp.maximum, logs)
+            log_norm = top + jnp.log2(sum(jnp.exp2(x - top) for x in logs))
+            comb[b, 0:1, :] = log_norm
+            comb[b, 1:2, :] = sum(
+                jnp.exp2(logs[d] - log_norm) * stat_all[d, h, b, 1:2, :] for d in range(n)
+            )
+        kt_ref[...] = jnp.transpose(k_ref[:, cols(h)].astype(F32)).astype(BF16)
+        acc_k[...] = jnp.zeros_like(acc_k)
+        acc_v[...] = jnp.zeros_like(acc_v)
+
+        @pl.loop(0, n)
+        def _(b):
+            q_b = q_all[b, :, cols(h)]
+            g_b = g_all[b, h]
+            dq_t = jnp.zeros((HD, rows), F32)
+            for j in range(key_tiles):
+                at = slice(j * TILE, (j + 1) * TILE)
+                p = jnp.exp2(logits(b, h, j) - comb[b, 0:1, :])
+                ds = (p * (dprobs(b, h, j) - comb[b, 1:2, :])).astype(BF16)
+                acc_v[at, :] += dot_nn(p.astype(BF16), g_b)
+                acc_k[at, :] += dot_nn(ds, q_b)
+                dq_t += dot_nn(kt_ref[:, at], ds)
+            part[b, h] = (dq_t * scale).astype(BF16)
+
+        key_full = acc_k[...] * scale
+        value_full = acc_v[...]
+        dk_ref[:, cols(h)] = key_full.astype(BF16)
+        dv_ref[:, cols(h)] = value_full.astype(BF16)
+        sq_all[z, 1, h] = jnp.sum(key_full * key_full, axis=0, keepdims=True)
+        sq_all[z, 2, h] = jnp.sum(value_full * value_full, axis=0, keepdims=True)
+
+    def chain_hop(h, way):
+        first = has_left if way == 0 else has_right
+
+        @pl.when((h >= 0) & (h < heads))
+        def _():
+            for i in range(1, n):
+                b = z + i if way == 0 else z - i
+
+                @pl.when((b >= 0) & (b < n))
+                def _():
+                    @pl.when(first)
+                    def _():
+                        chain_arrival(b, h).wait_recv()
+                        part[b, h] = (part[b, h].astype(F32) + chain[b, h].astype(F32)).astype(BF16)
+
+                    chain_copy(b, h, way).start()
+
+    def own_sum(h):
+        @pl.when((h >= 0) & (h < heads))
+        def _():
+            acc_q[...] = part[z, h].astype(F32)
+
+            @pl.when(has_left)
+            def _():
+                chain_arrival(z, h).wait_recv()
+                acc_q[...] += chain[z, h].astype(F32)
+
+            @pl.when(has_right)
+            def _():
+                chain_arrival(n, h).wait_recv()
+                acc_q[...] += chain[n, h].astype(F32)
+
+            query_full = jnp.transpose(acc_q[...])
+            dq_ref[:, cols(h)] = query_full.astype(BF16)
+            sq_all[z, 0, h] = jnp.sum(query_full * query_full, axis=0, keepdims=True)
+
+    lead = max(n - 2, 0)
+
+    @pl.loop(0, lead + heads + n)
+    def _(step):
+        t = step - lead
+        for s in range(1, n):
+            g_hop(s, t + (n - 1 - s))
+
+        @pl.when((t >= 0) & (t < heads))
+        def _():
+            first_pass(t)
+
+        @pl.when((t >= 1) & (t <= heads))
+        def _():
+            second_pass(t - 1)
+
+        chain_hop(t - 1 - z, 0)
+        chain_hop(t - 1 - (n - 1 - z), 1)
+        own_sum(t - 1 - jnp.maximum(z, n - 1 - z))
+
+    for i in range(1, n):
+        sq_copy(i).start()
+    for i in range(1, n):
+        sq_arrival(lax.rem(z + i, n)).wait_recv()
+    total = functools.reduce(jnp.add, [sq_all[d] for d in range(n)])
+    mean = jnp.sum(total, axis=-1, keepdims=True) / (n * rows * HD)
+    feat_ref[...] = jnp.broadcast_to(jnp.log(mean + 1e-06), feat_ref.shape)
+
+    for i in range(1, nh):
+        og_copy(i).wait_send()
+    for i in range(1, n):
+        sq_copy(i).wait_send()
+    both_ways(lambda way: q_copy(z, way).wait_send())
+    for s in range(1, n - 1):
+        @pl.when((z - s >= 0) & has_right)
+        def _():
+            q_copy(z - s, 0).wait_send()
+
+        @pl.when((z + s < n) & has_left)
+        def _():
+            q_copy(z + s, 1).wait_send()
+
+    @pl.loop(0, heads)
+    def _(h):
+        both_ways(lambda way: g_copy(z, h, way).wait_send())
+        for s in range(1, n - 1):
+            @pl.when((z - s >= 0) & has_right)
+            def _():
+                g_copy(z - s, h, 0).wait_send()
+
+            @pl.when((z + s < n) & has_left)
+            def _():
+                g_copy(z + s, h, 1).wait_send()
+        for i in range(1, n):
+            stat_copy(h, i).wait_send()
+
+            @pl.when(z + i < n)
+            def _():
+                chain_copy(z + i, h, 0).wait_send()
+
+            @pl.when(z - i >= 0)
+            def _():
+                chain_copy(z - i, h, 1).wait_send()
+
+
+def fused_bytes(n, nh, rows, width, feats):
+    block = rows * width * 2
+    return block * (6 + 3 * n + n + 1) + rows * feats * 2 * (1 + nh) + width * feats * nh * 2 + 2 * block
+
+
+def per_device(query_states, key_states, value_states, output_grad, w_out, key_list, key_count):
+    n = lax.axis_size("seq")
+    nh = lax.axis_size("head")
+    rows, width = query_states.shape[1:]
+    feats = output_grad.shape[2]
+    if n < 2 or fused_bytes(n, nh, rows, width, feats) > VMEM_BYTES * 3 // 4:
+        return gathered_plan(
+            query_states, key_states, value_states, output_grad, w_out, key_list, key_count
+        )
+    heads = width // HD
+    key_tiles = rows // TILE
+    tiles, slots = key_list.shape[1:]
+    own_tiles = lax.axis_index("seq") * key_tiles + jnp.arange(key_tiles)
+    live = jnp.arange(slots)[None, :] < key_count[0][:, None]
+    listed = (key_list[0][:, :, None] == own_tiles[None, None, :]) & live[:, :, None]
+    bias = jnp.where(jnp.any(listed, axis=1), 0.0, NEG_BIG).astype(F32)
+    bias = jnp.repeat(bias.reshape(n, key_tiles, key_tiles), TILE, axis=1).transpose(0, 2, 1)
+    wide = 256 if width % 256 == 0 else HD
+    vmem = pl.BlockSpec(memory_space=pltpu.VMEM)
+    dma = pltpu.SemaphoreType.DMA
+    block = jax.ShapeDtypeStruct((rows, width), BF16)
+    dq, dk, dv, feat = pl.pallas_call(
+        functools.partial(fused_kernel, n, nh),
+        out_shape=[block, block, block, jax.ShapeDtypeStruct((3, heads, 1, HD), F32)],
+        in_specs=[vmem] * 6,
+        out_specs=[vmem] * 4,
+        scratch_shapes=[
+            pltpu.VMEM((n, rows, width), BF16),
+            pltpu.VMEM((n, heads, rows, HD), BF16),
+            pltpu.VMEM((nh, rows, feats), BF16),
+            pltpu.VMEM((width // wide, rows, wide), F32),
+            pltpu.VMEM((n, heads, n, 2, rows), F32),
+            pltpu.VMEM((n, 2, rows), F32),
+            pltpu.VMEM((n, heads, HD, rows), BF16),
+            pltpu.VMEM((n + 1, heads, HD, rows), BF16),
+            pltpu.VMEM((HD, rows), BF16),
+            pltpu.VMEM((rows, HD), F32),
+            pltpu.VMEM((rows, HD), F32),
+            pltpu.VMEM((HD, rows), F32),
+            pltpu.VMEM((n, 3, heads, 1, HD), F32),
+            dma((nh,)), dma((nh,)),
+            dma((2, n)), dma((n,)),
+            dma((2, n, heads)), dma((n, heads)),
+            dma((heads, n)), dma((n, heads)),
+            dma((n, heads)), dma((n + 1, heads)),
+            dma((n,)), dma((n,)),
+        ],
+        compiler_params=pltpu.CompilerParams(
+            collective_id=0, has_side_effects=True, vmem_limit_bytes=VMEM_BYTES
+        ),
+        cost_estimate=pl.CostEstimate(
+            flops=14 * rows * rows * n * width + 2 * rows * width * feats * nh,
+            bytes_accessed=16 * rows * width,
+            transcendentals=2 * rows * rows * n * heads,
+        ),
+    )(query_states[0], key_states[0], value_states[0], output_grad[0], w_out, bias)
+    grad_features = jnp.transpose(feat[:, :, 0, 0])
+    return dq[None], dk[None], dv[None], grad_features[None]
+
+
 def solution(mesh):
     in_specs = (
         P(("grp", "clip"), "seq", "head"),

time: 463 us -> 180 us (0.39)
  waiting for transfers between devices: 260 us -> 0 us
  Pallas kernels: 0 us -> 169 us
  matrix products: 108 us -> 0 us
  local copies, waits for them, and re-layouts: 58.6 us -> 8.39 us
  between operations: 13.9 us -> 0.66 us
  blocking collectives: 10.4 us -> 0 us
  other arithmetic: 9.63 us -> 1.64 us
    pallas_call x0 -> x1, Pallas kernels: none -> 169 us  [per_device(): pl.pallas_call(functools.partial(fused_kernel, n, nh), out_shape=[block,...]
    all_gather x3 -> x0, waiting for transfers between devices: 164 us -> none  [the longest x1 59.2 us: per_device(): lax.all_gather(key_states, 'seq', axis=1, tiled=True)]
    dot_general x39 -> x0, matrix products: 108 us -> none  [the longest x6 20.2 us: head_step(): jnp.einsum('iqk,iqe->ike', dscore, query_head, preferred_element_type=jnp...]
    reduce_scatter x2 -> x0, waiting for transfers between devices: 94 us -> none  [the longest x1 61.6 us: per_device(): lax.psum_scatter(value_grad_buf.reshape(1, buf_rows, feat_width).astype(j...]
    reshape x2 -> x1, local copies, waits for them, and re-layouts: 26.6 us -> 0.64 us  [per_device(): jnp.repeat(bias.reshape(n, key_tiles, key_tiles), TILE, axis=1)]
    gather x2 -> x0, local copies, waits for them, and re-layouts: 11.1 us -> none  [the longest x1 5.55 us: attend(): key_sel = key_buf[buf_slots].reshape(tile_count, key_span, feat_width)]
    another operation x2 -> x0, local copies, waits for them, and re-layouts: 10.7 us -> none
    psum x1 -> x0, blocking collectives: 10.4 us -> none  [per_device(): total_sums = lax.psum(local_sums, 'seq')]
  transfers between devices with their start and end apart: 5 -> 0, of which waited for: 5 -> 0; matrix products, arithmetic and copies ran while one was open for 9% -> 0% of each run, Pallas kernels for 0% -> 0%
where the time goes in v1:
time: 180 us
  Pallas kernels  169 us (94%)
  local copies, waits for them, and re-layouts  8.39 us (5%)
    pallas_call x1, Pallas kernels, per_device(): pl.pallas_call(functools.partial(fused_kernel, n, nh), out_shape=[block,...  169 us
    unnamed x4, local copies, waits for them, and re-layouts  6.75 us

profile of v1, /device:TPU:0, one launch (start us, length us, event | category | flops | bytes accessed | tf_op | source)
XLA Modules:
  0.0 180.0 jit_solution(5447920073943162338)
XLA Ops:
  0.6 0.7 iota_compare_fusion
  1.4 0.9 and_reduce_fusion
  2.3 0.1 select_n.9
  2.4 0.1 broadcast_in_dim.28
  2.4 0.6 reshape.45
  3.1 169.3 %shard_map.102 = (bf16[512,768]{1,0:T(8,128)(2,1)}, bf16[512,768]{1,0:T(8,128)(2,1)}, bf16[512,768]{1,0:T(8,128)(2,1)}, f32[3,6,1,128]{3,2,1,0:T(1,128)}) custom-call(bf16[512,768]{1,0:T(8,128)(2,1)} %bitcast.24, bf16[512,768]{1,0:T(8,128)(2,1)} %bitcast.25, bf16[512,768]{1,0:T(8,128)(2,1)} %bitcast.26, bf16[512,1536]{1,0:T(8,128)(2,1)} %bitcast.23, ...), custom_call_target="tpu_custom_call" | custom-call | flops 13690208256 | bytes 6291456 | tf_op jit(solution)/shard_map/pallas_call | solution.py:511
  172.4 0.8 slice_reduce_fusion
  173.3 0.6 copy.16
  173.8 2.1 %copy.20 = bf16[1,512,768]{2,1,0:T(8,128)(2,1)} copy(bf16[1,512,768]{2,1,0:T(8,128)(2,1)} %bitcast.19) | data formatting | bytes 1572864
  175.9 2.1 %copy.21 = bf16[1,512,768]{2,1,0:T(8,128)(2,1)} copy(bf16[1,512,768]{2,1,0:T(8,128)(2,1)} %bitcast.18) | data formatting | bytes 1572864
  178.0 2.1 %copy.22 = bf16[1,512,768]{2,1,0:T(8,128)(2,1)} copy(bf16[1,512,768]{2,1,0:T(8,128)(2,1)} %bitcast.17) | data formatting | bytes 1572864
  (3 shorter events, 0.0 us)

commit v2 on v1

--- a/solution.py
+++ b/solution.py
@@ -177,11 +177,12 @@
 
 
 def fused_kernel(
-    n, nh, q_ref, k_ref, v_ref, og_ref, w_ref, bias_ref,
+    n, nh, list_ref, count_ref, q_ref, k_hbm, v_hbm, og_ref, w_hbm,
     dq_ref, dk_ref, dv_ref, feat_ref,
-    q_all, g_all, og_all, g_acc, stat_all, comb, part, chain, kt_ref, acc_k, acc_v, acc_q, sq_all,
-    og_send, og_recv, q_send, q_recv, g_send, g_recv, stat_send, stat_recv,
-    chain_send, chain_recv, sq_send, sq_recv,
+    k_ref, v_ref, w_ref, bias_ref, q_all, g_all, og_all, g_acc, probs, top_ref, inv_ref,
+    lse_all, eps_all, part, chain, kt_ref, acc_k, acc_v, acc_q, sq_all,
+    load_sem, og_send, og_recv, q_send, q_recv, g_send, g_recv, lse_send, lse_recv,
+    eps_send, eps_recv, chain_send, chain_recv, sq_send, sq_recv,
 ):
     z = lax.axis_index("seq")
     hx = lax.axis_index("head")
@@ -194,6 +195,15 @@
     has_left = z > 0
     has_right = z < n - 1
 
+    loads = [
+        pltpu.make_async_copy(src, dst, load_sem.at[i])
+        for i, (src, dst) in enumerate(
+            ((q_ref, q_all.at[z]), (og_ref, og_all.at[hx]), (w_hbm, w_ref), (k_hbm, k_ref), (v_hbm, v_ref))
+        )
+    ]
+    for load in loads:
+        load.start()
+
     def remote(src, dst, ssem, rsem, axis, idx):
         return pltpu.make_async_remote_copy(
             src_ref=src, dst_ref=dst, send_sem=ssem, recv_sem=rsem,
@@ -216,17 +226,26 @@
     def og_arrival(j):
         return remote(og_all.at[j], og_all.at[j], og_send.at[0], og_recv.at[j], "head", hx)
 
+    def q_own(way):
+        return remote(q_ref, q_all.at[z], q_send.at[way, z], q_recv.at[z], "seq", z + (1 - 2 * way))
+
     def q_copy(b, way):
         return remote(q_all.at[b], q_all.at[b], q_send.at[way, b], q_recv.at[b], "seq", z + (1 - 2 * way))
 
     def g_copy(b, h, way):
         return remote(g_all.at[b, h], g_all.at[b, h], g_send.at[way, b, h], g_recv.at[b, h], "seq", z + (1 - 2 * way))
 
-    def stat_copy(h, i):
-        return remote(stat_all.at[z, h], stat_all.at[z, h], stat_send.at[h, i], stat_recv.at[z, h], "seq", lax.rem(z + i, n))
-
-    def stat_arrival(d, h):
-        return remote(stat_all.at[d, h], stat_all.at[d, h], stat_send.at[h, 0], stat_recv.at[d, h], "seq", z)
+    def lse_copy(i):
+        return remote(lse_all.at[z], lse_all.at[z], lse_send.at[i], lse_recv.at[z], "seq", lax.rem(z + i, n))
+
+    def lse_arrival(d):
+        return remote(lse_all.at[d], lse_all.at[d], lse_send.at[0], lse_recv.at[d], "seq", z)
+
+    def eps_copy(h, i):
+        return remote(eps_all.at[z, h], eps_all.at[z, h], eps_send.at[h, i], eps_recv.at[z, h], "seq", lax.rem(z + i, n))
+
+    def eps_arrival(d, h):
+        return remote(eps_all.at[d, h], eps_all.at[d, h], eps_send.at[h, 0], eps_recv.at[d, h], "seq", z)
 
     def chain_copy(b, h, way):
         slot = b if way == 0 else jnp.where(b == z - 1, n, b)
@@ -252,8 +271,17 @@
 
     for i in range(1, nh):
         og_copy(i).start()
-    q_all[z] = q_ref[...]
-    both_ways(lambda way: q_copy(z, way).start())
+    both_ways(lambda way: q_own(way).start())
+
+    tiles, slots = list_ref.shape
+    for i in range(tiles):
+        for j in range(key_tiles):
+            bias = jnp.float32(NEG_BIG)
+            for m in range(slots):
+                hit = (list_ref[i, m] == z * key_tiles + j) & (m < count_ref[0, i])
+                bias = jnp.where(hit, jnp.float32(0.0), bias)
+            at = (i % key_tiles) * TILE
+            bias_ref[i // key_tiles, j, :, at : at + TILE] = jnp.full((1, TILE), bias, F32)
 
     wide = 256 if width % 256 == 0 else HD
 
@@ -269,7 +297,9 @@
             else:
                 g_acc[c] = term
 
-    features_of(og_ref, hx, False)
+    for load in loads:
+        load.wait()
+    features_of(og_all.at[hx], hx, False)
 
     def q_hop(s):
         @pl.when(z - s >= 0)
@@ -288,9 +318,42 @@
             def _():
                 q_copy(z + s, 1).start()
 
+    def softmax_rows(b):
+        @pl.loop(0, heads)
+        def _(h):
+            ts = []
+            for j in range(key_tiles):
+                t = dot_nt(k_ref[j * TILE : (j + 1) * TILE, cols(h)], q_all[b, :, cols(h)])
+                ts.append(t * scale2 + bias_ref[b, j])
+            top = functools.reduce(jnp.maximum, [jnp.max(t, axis=0, keepdims=True) for t in ts])
+            total = jnp.zeros((1, rows), F32)
+            for j in range(key_tiles):
+                p = jnp.exp2(ts[j] - top)
+                total += jnp.sum(p, axis=0, keepdims=True)
+                probs[b, h, j * TILE : (j + 1) * TILE, :] = p.astype(BF16)
+            top_ref[h, b] = top
+            inv_ref[h, b] = 1.0 / total
+            lse_all[z, h, b] = top + jnp.log2(total)
+
+    def softmax_at(s):
+        @pl.when(z - s >= 0)
+        def _():
+            softmax_rows(z - s)
+
+        @pl.when(z + s < n)
+        def _():
+            softmax_rows(z + s)
+
+    @pl.loop(0, heads)
+    def _(h):
+        kt_ref[h] = jnp.transpose(k_ref[:, cols(h)].astype(F32)).astype(BF16)
+
+    softmax_rows(z)
     early = min(2, n - 1)
     for s in range(1, early + 1):
         q_hop(s)
+        if s < early:
+            softmax_at(s)
     for i in range(1, nh):
         j = lax.rem(hx + i, nh)
         og_arrival(j).wait_recv()
@@ -299,8 +362,12 @@
         lo = h * HD
         g_all[z, h] = g_acc[lo // wide, :, lo % wide : lo % wide + HD].astype(BF16)
         both_ways(lambda way: g_copy(z, h, way).start())
+    softmax_at(early)
     for s in range(early + 1, n):
         q_hop(s)
+        softmax_at(s)
+    for i in range(1, n):
+        lse_copy(i).start()
 
     def g_hop(s, h):
         @pl.when((h >= 0) & (h < heads))
@@ -321,57 +388,44 @@
                     def _():
                         g_copy(z + s, h, 1).start()
 
-    def logits(b, h, j):
-        t = dot_nt(k_ref[j * TILE : (j + 1) * TILE, cols(h)], q_all[b, :, cols(h)])
-        return t * scale2 + bias_ref[b, j : j + 1, :]
-
     def dprobs(b, h, j):
         return dot_nt(v_ref[j * TILE : (j + 1) * TILE, cols(h)], g_all[b, h])
 
     def first_pass(h):
         @pl.loop(0, n)
         def _(b):
-            ts = [logits(b, h, j) for j in range(key_tiles)]
-            top = functools.reduce(jnp.maximum, [jnp.max(t, axis=0, keepdims=True) for t in ts])
-            total = jnp.zeros((1, rows), F32)
             eps = jnp.zeros((1, rows), F32)
             for j in range(key_tiles):
-                p = jnp.exp2(ts[j] - top)
-                total += jnp.sum(p, axis=0, keepdims=True)
+                p = probs[b, h, j * TILE : (j + 1) * TILE, :].astype(F32)
                 eps += jnp.sum(p * dprobs(b, h, j), axis=0, keepdims=True)
-            stat_all[z, h, b, 0:1, :] = top + jnp.log2(total)
-            stat_all[z, h, b, 1:2, :] = eps / total
+            eps_all[z, h, b] = eps * inv_ref[h, b]
 
         for i in range(1, n):
-            stat_copy(h, i).start()
+            eps_copy(h, i).start()
 
     def second_pass(h):
         for i in range(1, n):
-            stat_arrival(lax.rem(z + i, n), h).wait_recv()
-        for b in range(n):
-            logs = [stat_all[d, h, b, 0:1, :] for d in range(n)]
+            eps_arrival(lax.rem(z + i, n), h).wait_recv()
+        acc_k[...] = jnp.zeros_like(acc_k)
+        acc_v[...] = jnp.zeros_like(acc_v)
+
+        @pl.loop(0, n)
+        def _(b):
+            logs = [lse_all[d, h, b] for d in range(n)]
             top = functools.reduce(jnp.maximum, logs)
             log_norm = top + jnp.log2(sum(jnp.exp2(x - top) for x in logs))
-            comb[b, 0:1, :] = log_norm
-            comb[b, 1:2, :] = sum(
-                jnp.exp2(logs[d] - log_norm) * stat_all[d, h, b, 1:2, :] for d in range(n)
-            )
-        kt_ref[...] = jnp.transpose(k_ref[:, cols(h)].astype(F32)).astype(BF16)
-        acc_k[...] = jnp.zeros_like(acc_k)
-        acc_v[...] = jnp.zeros_like(acc_v)
-
-        @pl.loop(0, n)
-        def _(b):
+            delta = sum(jnp.exp2(logs[d] - log_norm) * eps_all[d, h, b] for d in range(n))
+            share = jnp.exp2(top_ref[h, b] - log_norm)
             q_b = q_all[b, :, cols(h)]
             g_b = g_all[b, h]
             dq_t = jnp.zeros((HD, rows), F32)
             for j in range(key_tiles):
                 at = slice(j * TILE, (j + 1) * TILE)
-                p = jnp.exp2(logits(b, h, j) - comb[b, 0:1, :])
-                ds = (p * (dprobs(b, h, j) - comb[b, 1:2, :])).astype(BF16)
+                p = probs[b, h, at, :].astype(F32) * share
+                ds = (p * (dprobs(b, h, j) - delta)).astype(BF16)
                 acc_v[at, :] += dot_nn(p.astype(BF16), g_b)
                 acc_k[at, :] += dot_nn(ds, q_b)
-                dq_t += dot_nn(kt_ref[:, at], ds)
+                dq_t += dot_nn(kt_ref[h, :, at], ds)
             part[b, h] = (dq_t * scale).astype(BF16)
 
         key_full = acc_k[...] * scale
@@ -429,6 +483,11 @@
         def _():
             first_pass(t)
 
+        @pl.when(t == 1)
+        def _():
+            for i in range(1, n):
+                lse_arrival(lax.rem(z + i, n)).wait_recv()
+
         @pl.when((t >= 1) & (t <= heads))
         def _():
             second_pass(t - 1)
@@ -443,13 +502,17 @@
         sq_arrival(lax.rem(z + i, n)).wait_recv()
     total = functools.reduce(jnp.add, [sq_all[d] for d in range(n)])
     mean = jnp.sum(total, axis=-1, keepdims=True) / (n * rows * HD)
-    feat_ref[...] = jnp.broadcast_to(jnp.log(mean + 1e-06), feat_ref.shape)
+    logs = jnp.log(mean + 1e-06)
+    lane = lax.broadcasted_iota(jnp.int32, (1, HD), 1)
+    for h in range(heads):
+        feat_ref[h : h + 1, :] = sum(jnp.where(lane == j, logs[j, h], 0.0) for j in range(3))
 
     for i in range(1, nh):
         og_copy(i).wait_send()
     for i in range(1, n):
         sq_copy(i).wait_send()
-    both_ways(lambda way: q_copy(z, way).wait_send())
+        lse_copy(i).wait_send()
+    both_ways(lambda way: q_own(way).wait_send())
     for s in range(1, n - 1):
         @pl.when((z - s >= 0) & has_right)
         def _():
@@ -471,7 +534,7 @@
             def _():
                 g_copy(z + s, h, 1).wait_send()
         for i in range(1, n):
-            stat_copy(h, i).wait_send()
+            eps_copy(h, i).wait_send()
 
             @pl.when(z + i < n)
             def _():
@@ -480,11 +543,19 @@
             @pl.when(z - i >= 0)
             def _():
                 chain_copy(z - i, h, 1).wait_send()
+
+
+def finish_kernel(dq_in, dk_in, dv_in, feat_in, dq_ref, dk_ref, dv_ref, feat_ref):
+    dq_ref[...] = dq_in[...]
+    dk_ref[...] = dk_in[...]
+    dv_ref[...] = dv_in[...]
+    feat_ref[...] = feat_in[:, : feat_ref.shape[1]]
 
 
 def fused_bytes(n, nh, rows, width, feats):
     block = rows * width * 2
-    return block * (6 + 3 * n + n + 1) + rows * feats * 2 * (1 + nh) + width * feats * nh * 2 + 2 * block
+    kept = n * (width // HD) * rows * rows * 2
+    return block * (5 + 3 * n + n + 1) + rows * feats * 2 * nh + width * feats * nh * 2 + 2 * block + kept
 
 
 def per_device(query_states, key_states, value_states, output_grad, w_out, key_list, key_count):
@@ -498,38 +569,41 @@
         )
     heads = width // HD
     key_tiles = rows // TILE
-    tiles, slots = key_list.shape[1:]
-    own_tiles = lax.axis_index("seq") * key_tiles + jnp.arange(key_tiles)
-    live = jnp.arange(slots)[None, :] < key_count[0][:, None]
-    listed = (key_list[0][:, :, None] == own_tiles[None, None, :]) & live[:, :, None]
-    bias = jnp.where(jnp.any(listed, axis=1), 0.0, NEG_BIG).astype(F32)
-    bias = jnp.repeat(bias.reshape(n, key_tiles, key_tiles), TILE, axis=1).transpose(0, 2, 1)
     wide = 256 if width % 256 == 0 else HD
     vmem = pl.BlockSpec(memory_space=pltpu.VMEM)
     dma = pltpu.SemaphoreType.DMA
     block = jax.ShapeDtypeStruct((rows, width), BF16)
     dq, dk, dv, feat = pl.pallas_call(
         functools.partial(fused_kernel, n, nh),
-        out_shape=[block, block, block, jax.ShapeDtypeStruct((3, heads, 1, HD), F32)],
-        in_specs=[vmem] * 6,
+        out_shape=[block, block, block, jax.ShapeDtypeStruct((heads, HD), F32)],
+        in_specs=[pl.BlockSpec(memory_space=pltpu.SMEM)] * 2 + [pl.BlockSpec(memory_space=pl.ANY)] * 5,
         out_specs=[vmem] * 4,
         scratch_shapes=[
+            pltpu.VMEM((rows, width), BF16),
+            pltpu.VMEM((rows, width), BF16),
+            pltpu.VMEM((width, feats * nh), BF16),
+            pltpu.VMEM((n, key_tiles, 1, rows), F32),
             pltpu.VMEM((n, rows, width), BF16),
             pltpu.VMEM((n, heads, rows, HD), BF16),
             pltpu.VMEM((nh, rows, feats), BF16),
             pltpu.VMEM((width // wide, rows, wide), F32),
-            pltpu.VMEM((n, heads, n, 2, rows), F32),
-            pltpu.VMEM((n, 2, rows), F32),
+            pltpu.VMEM((n, heads, rows, rows), BF16),
+            pltpu.VMEM((heads, n, 1, rows), F32),
+            pltpu.VMEM((heads, n, 1, rows), F32),
+            pltpu.VMEM((n, heads, n, 1, rows), F32),
+            pltpu.VMEM((n, heads, n, 1, rows), F32),
             pltpu.VMEM((n, heads, HD, rows), BF16),
             pltpu.VMEM((n + 1, heads, HD, rows), BF16),
-            pltpu.VMEM((HD, rows), BF16),
+            pltpu.VMEM((heads, HD, rows), BF16),
             pltpu.VMEM((rows, HD), F32),
             pltpu.VMEM((rows, HD), F32),
             pltpu.VMEM((HD, rows), F32),
             pltpu.VMEM((n, 3, heads, 1, HD), F32),
+            dma((5,)),
             dma((nh,)), dma((nh,)),
             dma((2, n)), dma((n,)),
             dma((2, n, heads)), dma((n, heads)),
+            dma((n,)), dma((n,)),
             dma((heads, n)), dma((n, heads)),
             dma((n, heads)), dma((n + 1, heads)),
             dma((n,)), dma((n,)),
@@ -542,8 +616,13 @@
             bytes_accessed=16 * rows * width,
             transcendentals=2 * rows * rows * n * heads,
         ),
-    )(query_states[0], key_states[0], value_states[0], output_grad[0], w_out, bias)
-    grad_features = jnp.transpose(feat[:, :, 0, 0])
+    )(key_list[0], key_count, query_states[0], key_states[0], value_states[0], output_grad[0], w_out)
+    dq, dk, dv, grad_features = pl.pallas_call(
+        finish_kernel,
+        out_shape=[block, block, block, jax.ShapeDtypeStruct((heads, 3), F32)],
+        in_specs=[vmem] * 4,
+        out_specs=[vmem] * 4,
+    )(dq, dk, dv, feat)
     return dq[None], dk[None], dv[None], grad_features[None]
 
 

time: 180 us -> 171 us (0.950)
  local copies, waits for them, and re-layouts: 8.39 us -> 1.3 us
    unnamed x4 -> x1, local copies, waits for them, and re-layouts: 6.75 us -> 1.3 us
    pallas_call x1, Pallas kernels: 169 us -> 166 us  [per_device(): pl.pallas_call(functools.partial(fused_kernel, n, nh), out_shape=[block,...]
    pallas_call x0 -> x1, Pallas kernels: none -> 3.06 us  [per_device(): pl.pallas_call(finish_kernel, out_shape=[block, block, block, jax.ShapeDt...]
where the time goes in v2:
time: 171 us
  Pallas kernels  169 us (99%)
    pallas_call x1, Pallas kernels, per_device(): pl.pallas_call(functools.partial(fused_kernel, n, nh), out_shape=[block,...  166 us

profile of v2, /device:TPU:0, one launch (start us, length us, event | category | flops | bytes accessed | tf_op | source)
XLA Modules:
  0.0 171.2 jit_solution(4080450835622967785)
XLA Ops:
  0.6 166.2 %shard_map.102 = (bf16[512,768]{1,0:T(8,128)(2,1)}, bf16[512,768]{1,0:T(8,128)(2,1)}, bf16[512,768]{1,0:T(8,128)(2,1)}, f32[6,128]{1,0:T(8,128)}) custom-call(s32[8,8]{1,0:T(8,128)} %bitcast.17, s32[1,8]{1,0:T(1,128)} %count_ref.1, bf16[512,768]{1,0:T(8,128)(2,1)} %bitcast.11, bf16[512,768]{1,0:T(8,128)(2,1)} %bitcast.12, bf16[512,768]{1,0:T(8,128)(2,1)} %bitcast.13, ...), custom_call_target="tpu_custom_call" | custom-call | flops 13690208256 | bytes 6291456 | tf_op jit(solution)/shard_map/pallas_call | solution.py:576
  166.8 3.1 %shard_map.103 = (bf16[512,768]{1,0:T(8,128)(2,1)}, bf16[512,768]{1,0:T(8,128)(2,1)}, bf16[512,768]{1,0:T(8,128)(2,1)}, f32[6,3]{1,0:T(8,128)}) custom-call(bf16[512,768]{1,0:T(8,128)(2,1)} %get-tuple-element.12.dq_in, bf16[512,768]{1,0:T(8,128)(2,1)} %get-tuple-element.13.dk_in, bf16[512,768]{1,0:T(8,128)(2,1)} %get-tuple-element.14.dv_in, ...), custom_call_target="tpu_custom_call" | custom-call | tf_op jit(solution)/shard_map/pallas_call | solution.py:620
  169.9 1.3 copy.12

commit v3 on v2

--- a/solution.py
+++ b/solution.py
@@ -177,11 +177,11 @@
 
 
 def fused_kernel(
-    n, nh, list_ref, count_ref, q_ref, k_hbm, v_hbm, og_ref, w_hbm,
+    n, nh, gc, list_ref, count_ref, q_ref, k_hbm, v_hbm, og_ref, w_hbm,
     dq_ref, dk_ref, dv_ref, feat_ref,
     k_ref, v_ref, w_ref, bias_ref, q_all, g_all, og_all, g_acc, probs, top_ref, inv_ref,
     lse_all, eps_all, part, chain, kt_ref, acc_k, acc_v, acc_q, sq_all,
-    load_sem, og_send, og_recv, q_send, q_recv, g_send, g_recv, lse_send, lse_recv,
+    guest_out, guest_in, guest_send, guest_recv, back_send, back_recv, load_sem, og_send, og_recv, q_send, q_recv, g_send, g_recv, lse_send, lse_recv,
     eps_send, eps_recv, chain_send, chain_recv, sq_send, sq_recv,
 ):
     z = lax.axis_index("seq")
@@ -194,11 +194,24 @@
     scale2 = scale * math.log2(math.e)
     has_left = z > 0
     has_right = z < n - 1
+    gw = gc * HD
+    is_end = (z == 0) | (z == n - 1)
+    host_low, host_high = z == 1, z == n - 2
+    is_host = (host_low | host_high) if gc else z < 0
+    guest = jnp.where(host_low, 0, n - 1)
+    host_of = jnp.where(z == 0, 1, n - 2)
+
+    def inner(d):
+        return (d > 0) & (d < n - 1)
+
+    def may_go(way, guest_part):
+        to = z + (1 - 2 * way)
+        return inner(to) if guest_part else (to >= 0) & (to < n)
 
     loads = [
         pltpu.make_async_copy(src, dst, load_sem.at[i])
         for i, (src, dst) in enumerate(
-            ((q_ref, q_all.at[z]), (og_ref, og_all.at[hx]), (w_hbm, w_ref), (k_hbm, k_ref), (v_hbm, v_ref))
+            ((q_ref, q_all.at[z]), (og_ref, og_all.at[hx]), (w_hbm, w_ref), (k_hbm, k_ref.at[:, 0:width]), (v_hbm, v_ref.at[:, 0:width]))
         )
     ]
     for load in loads:
@@ -226,26 +239,69 @@
     def og_arrival(j):
         return remote(og_all.at[j], og_all.at[j], og_send.at[0], og_recv.at[j], "head", hx)
 
-    def q_own(way):
-        return remote(q_ref, q_all.at[z], q_send.at[way, z], q_recv.at[z], "seq", z + (1 - 2 * way))
-
-    def q_copy(b, way):
-        return remote(q_all.at[b], q_all.at[b], q_send.at[way, b], q_recv.at[b], "seq", z + (1 - 2 * way))
+    q_parts = [(0, gw), (gw, width - gw)] if gc else [(0, width)]
+
+    def q_own(way, p):
+        at = pl.ds(*q_parts[p])
+        return remote(q_ref.at[:, at], q_all.at[z, :, at], q_send.at[way, z, p], q_recv.at[z, p], "seq", z + (1 - 2 * way))
+
+    def q_copy(b, way, p):
+        ref = q_all.at[b, :, pl.ds(*q_parts[p])]
+        return remote(ref, ref, q_send.at[way, b, p], q_recv.at[b, p], "seq", z + (1 - 2 * way))
+
+    def lend(i):
+        src, dst = ((k_hbm, k_ref), (v_hbm, v_ref))[i]
+        return remote(src.at[:, 0:gw], dst.at[:, width : width + gw], guest_send.at[i], guest_recv.at[i], "seq", host_of)
+
+    def lent(i):
+        ref = (k_ref, v_ref)[i].at[:, width : width + gw]
+        return remote(ref, ref, guest_send.at[i], guest_recv.at[i], "seq", z)
+
+    def back_copy(h):
+        return remote(guest_out.at[h], guest_in.at[h], back_send.at[h], back_recv.at[h], "seq", guest)
+
+    def back_arrival(h):
+        return remote(guest_in.at[h], guest_in.at[h], back_send.at[h], back_recv.at[h], "seq", z)
 
     def g_copy(b, h, way):
         return remote(g_all.at[b, h], g_all.at[b, h], g_send.at[way, b, h], g_recv.at[b, h], "seq", z + (1 - 2 * way))
 
-    def lse_copy(i):
-        return remote(lse_all.at[z], lse_all.at[z], lse_send.at[i], lse_recv.at[z], "seq", lax.rem(z + i, n))
-
-    def lse_arrival(d):
-        return remote(lse_all.at[d], lse_all.at[d], lse_send.at[0], lse_recv.at[d], "seq", z)
-
-    def eps_copy(h, i):
-        return remote(eps_all.at[z, h], eps_all.at[z, h], eps_send.at[h, i], eps_recv.at[z, h], "seq", lax.rem(z + i, n))
+    def lse_ref(d, p):
+        return lse_all.at[d, 0:gc] if p else lse_all.at[d, gc:heads]
+
+    def lse_copy(d, i, p, k):
+        return remote(lse_ref(d, p), lse_ref(d, p), lse_send.at[i, k], lse_recv.at[d, p], "seq", lax.rem(z + i, n))
+
+    def lse_arrival(d, p):
+        return remote(lse_ref(d, p), lse_ref(d, p), lse_send.at[0, 0], lse_recv.at[d, p], "seq", z)
+
+    def eps_copy(d, h, i, k):
+        return remote(eps_all.at[d, h], eps_all.at[d, h], eps_send.at[h, i, k], eps_recv.at[d, h], "seq", lax.rem(z + i, n))
 
     def eps_arrival(d, h):
-        return remote(eps_all.at[d, h], eps_all.at[d, h], eps_send.at[h, 0], eps_recv.at[d, h], "seq", z)
+        return remote(eps_all.at[d, h], eps_all.at[d, h], eps_send.at[h, 0, 0], eps_recv.at[d, h], "seq", z)
+
+    def lse_sends(act):
+        for i in range(1, n):
+            act(lse_copy(z, i, 0, 0))
+            if gc:
+                @pl.when(inner(z) & inner(lax.rem(z + i, n)))
+                def _():
+                    act(lse_copy(z, i, 1, 1))
+
+                    @pl.when(is_host)
+                    def _():
+                        act(lse_copy(guest, i, 1, 2))
+
+    def eps_sends(h, act):
+        for i in range(1, n):
+            @pl.when((h >= gc) | (inner(z) & inner(lax.rem(z + i, n))))
+            def _():
+                act(eps_copy(z, h, i, 0))
+
+            @pl.when((h < gc) & is_host & inner(lax.rem(z + i, n)))
+            def _():
+                act(eps_copy(guest, h, i, 1))
 
     def chain_copy(b, h, way):
         slot = b if way == 0 else jnp.where(b == z - 1, n, b)
@@ -260,28 +316,44 @@
     def sq_arrival(d):
         return remote(sq_all.at[d], sq_all.at[d], sq_send.at[0], sq_recv.at[d], "seq", z)
 
-    def both_ways(copy_of):
-        @pl.when(has_right)
-        def _():
-            copy_of(0)
-
-        @pl.when(has_left)
-        def _():
-            copy_of(1)
+    def q_own_all(act):
+        for p in range(len(q_parts)):
+            for way in range(2):
+                @pl.when(may_go(way, gc > 0 and p == 0))
+                def _():
+                    act(q_own(way, p))
+
+    def q_on(s, act):
+        for way, b in ((0, z - s), (1, z + s)):
+            for p in range(len(q_parts)):
+                @pl.when((b >= 0) & (b < n) & may_go(way, gc > 0 and p == 0))
+                def _():
+                    act(q_copy(b, way, p))
+
+    def g_sends(b, h, way, act):
+        @pl.when((b >= 0) & (b < n) & may_go(way, False) & ((h >= gc) | may_go(way, True)))
+        def _():
+            act(g_copy(b, h, way))
 
     for i in range(1, nh):
         og_copy(i).start()
-    both_ways(lambda way: q_own(way).start())
+    q_own_all(lambda c: c.start())
+    if gc:
+        @pl.when(is_end)
+        def _():
+            lend(0).start()
+            lend(1).start()
 
     tiles, slots = list_ref.shape
     for i in range(tiles):
         for j in range(key_tiles):
-            bias = jnp.float32(NEG_BIG)
-            for m in range(slots):
-                hit = (list_ref[i, m] == z * key_tiles + j) & (m < count_ref[0, i])
-                bias = jnp.where(hit, jnp.float32(0.0), bias)
             at = (i % key_tiles) * TILE
-            bias_ref[i // key_tiles, j, :, at : at + TILE] = jnp.full((1, TILE), bias, F32)
+            for k, owner in enumerate((z, guest) if gc else (z,)):
+                bias = jnp.float32(NEG_BIG)
+                for m in range(slots):
+                    hit = (list_ref[i, m] == owner * key_tiles + j) & (m < count_ref[0, i])
+                    bias = jnp.where(hit, jnp.float32(0.0), bias)
+                bias_ref[k, i // key_tiles, j, :, at : at + TILE] = jnp.full((1, TILE), bias, F32)
 
     wide = 256 if width % 256 == 0 else HD
 
@@ -302,53 +374,53 @@
     features_of(og_all.at[hx], hx, False)
 
     def q_hop(s):
-        @pl.when(z - s >= 0)
-        def _():
-            q_copy(z - s, 0).wait_recv()
-
-            @pl.when(has_right)
-            def _():
-                q_copy(z - s, 0).start()
-
-        @pl.when(z + s < n)
-        def _():
-            q_copy(z + s, 1).wait_recv()
-
-            @pl.when(has_left)
-            def _():
-                q_copy(z + s, 1).start()
-
-    def softmax_rows(b):
-        @pl.loop(0, heads)
-        def _(h):
+        for way, b in ((0, z - s), (1, z + s)):
+            @pl.when((b >= 0) & (b < n))
+            def _():
+                for p in range(len(q_parts)):
+                    @pl.when(inner(z) if gc > 0 and p == 0 else z >= 0)
+                    def _():
+                        q_copy(b, way, p).wait_recv()
+
+                        @pl.when(may_go(way, gc > 0 and p == 0))
+                        def _():
+                            q_copy(b, way, p).start()
+
+    first_head = jnp.where(is_end, gc, 0)
+
+    def softmax_rows(b, low, high):
+        @pl.loop(low, high)
+        def _(v):
+            mine = v < heads
+            h = jnp.where(mine, v, v - heads)
             ts = []
             for j in range(key_tiles):
-                t = dot_nt(k_ref[j * TILE : (j + 1) * TILE, cols(h)], q_all[b, :, cols(h)])
-                ts.append(t * scale2 + bias_ref[b, j])
+                t = dot_nt(k_ref[j * TILE : (j + 1) * TILE, cols(v)], q_all[b, :, cols(h)])
+                ts.append(t * scale2 + bias_ref[jnp.where(mine, 0, 1), b, j])
             top = functools.reduce(jnp.maximum, [jnp.max(t, axis=0, keepdims=True) for t in ts])
             total = jnp.zeros((1, rows), F32)
             for j in range(key_tiles):
                 p = jnp.exp2(ts[j] - top)
                 total += jnp.sum(p, axis=0, keepdims=True)
-                probs[b, h, j * TILE : (j + 1) * TILE, :] = p.astype(BF16)
-            top_ref[h, b] = top
-            inv_ref[h, b] = 1.0 / total
-            lse_all[z, h, b] = top + jnp.log2(total)
+                probs[b, v, j * TILE : (j + 1) * TILE, :] = p.astype(BF16)
+            top_ref[v, b] = top
+            inv_ref[v, b] = 1.0 / total
+            lse_all[jnp.where(mine, z, guest), h, b] = top + jnp.log2(total)
 
     def softmax_at(s):
         @pl.when(z - s >= 0)
         def _():
-            softmax_rows(z - s)
+            softmax_rows(z - s, first_head, heads)
 
         @pl.when(z + s < n)
         def _():
-            softmax_rows(z + s)
+            softmax_rows(z + s, first_head, heads)
 
     @pl.loop(0, heads)
     def _(h):
         kt_ref[h] = jnp.transpose(k_ref[:, cols(h)].astype(F32)).astype(BF16)
 
-    softmax_rows(z)
+    softmax_rows(z, first_head, heads)
     early = min(2, n - 1)
     for s in range(1, early + 1):
         q_hop(s)
@@ -361,111 +433,160 @@
     for h in range(heads):
         lo = h * HD
         g_all[z, h] = g_acc[lo // wide, :, lo % wide : lo % wide + HD].astype(BF16)
-        both_ways(lambda way: g_copy(z, h, way).start())
+        for way in range(2):
+            g_sends(z, h, way, lambda c: c.start())
     softmax_at(early)
     for s in range(early + 1, n):
         q_hop(s)
         softmax_at(s)
-    for i in range(1, n):
-        lse_copy(i).start()
+    if gc:
+        @pl.when(is_host)
+        def _():
+            lent(0).wait_recv()
+            lent(1).wait_recv()
+
+            @pl.loop(heads, heads + gc)
+            def _(v):
+                kt_ref[v] = jnp.transpose(k_ref[:, cols(v)].astype(F32)).astype(BF16)
+
+            @pl.loop(0, n)
+            def _(b):
+                softmax_rows(b, heads, heads + gc)
+
+    lse_sends(lambda c: c.start())
 
     def g_hop(s, h):
-        @pl.when((h >= 0) & (h < heads))
-        def _():
-            @pl.when(z - s >= 0)
-            def _():
-                g_copy(z - s, h, 0).wait_recv()
+        for way, b in ((0, z - s), (1, z + s)):
+            @pl.when((h >= 0) & (h < heads) & (b >= 0) & (b < n) & ((h >= gc) | inner(z)))
+            def _():
+                g_copy(b, h, way).wait_recv()
                 if s < n - 1:
-                    @pl.when(has_right)
-                    def _():
-                        g_copy(z - s, h, 0).start()
-
-            @pl.when(z + s < n)
-            def _():
-                g_copy(z + s, h, 1).wait_recv()
-                if s < n - 1:
-                    @pl.when(has_left)
-                    def _():
-                        g_copy(z + s, h, 1).start()
-
-    def dprobs(b, h, j):
-        return dot_nt(v_ref[j * TILE : (j + 1) * TILE, cols(h)], g_all[b, h])
+                    g_sends(b, h, way, lambda c: c.start())
+
+    def dprobs(b, v, h, j):
+        return dot_nt(v_ref[j * TILE : (j + 1) * TILE, cols(v)], g_all[b, h])
+
+    def holders(h):
+        return jnp.where(h < gc, jnp.where(is_end, 0, jnp.where(is_host, 2, 1)), 1)
 
     def first_pass(h):
-        @pl.loop(0, n)
-        def _(b):
-            eps = jnp.zeros((1, rows), F32)
-            for j in range(key_tiles):
-                p = probs[b, h, j * TILE : (j + 1) * TILE, :].astype(F32)
-                eps += jnp.sum(p * dprobs(b, h, j), axis=0, keepdims=True)
-            eps_all[z, h, b] = eps * inv_ref[h, b]
-
-        for i in range(1, n):
-            eps_copy(h, i).start()
+        @pl.loop(0, holders(h))
+        def _(k):
+            v = h + k * heads
+            owner = jnp.where(k == 0, z, guest)
+
+            @pl.loop(0, n)
+            def _(b):
+                eps = jnp.zeros((1, rows), F32)
+                for j in range(key_tiles):
+                    p = probs[b, v, j * TILE : (j + 1) * TILE, :].astype(F32)
+                    eps += jnp.sum(p * dprobs(b, v, h, j), axis=0, keepdims=True)
+                eps_all[owner, h, b] = eps * inv_ref[v, b]
+
+        eps_sends(h, lambda c: c.start())
 
     def second_pass(h):
         for i in range(1, n):
-            eps_arrival(lax.rem(z + i, n), h).wait_recv()
-        acc_k[...] = jnp.zeros_like(acc_k)
-        acc_v[...] = jnp.zeros_like(acc_v)
-
-        @pl.loop(0, n)
-        def _(b):
-            logs = [lse_all[d, h, b] for d in range(n)]
-            top = functools.reduce(jnp.maximum, logs)
-            log_norm = top + jnp.log2(sum(jnp.exp2(x - top) for x in logs))
-            delta = sum(jnp.exp2(logs[d] - log_norm) * eps_all[d, h, b] for d in range(n))
-            share = jnp.exp2(top_ref[h, b] - log_norm)
-            q_b = q_all[b, :, cols(h)]
-            g_b = g_all[b, h]
-            dq_t = jnp.zeros((HD, rows), F32)
-            for j in range(key_tiles):
-                at = slice(j * TILE, (j + 1) * TILE)
-                p = probs[b, h, at, :].astype(F32) * share
-                ds = (p * (dprobs(b, h, j) - delta)).astype(BF16)
-                acc_v[at, :] += dot_nn(p.astype(BF16), g_b)
-                acc_k[at, :] += dot_nn(ds, q_b)
-                dq_t += dot_nn(kt_ref[h, :, at], ds)
-            part[b, h] = (dq_t * scale).astype(BF16)
-
-        key_full = acc_k[...] * scale
-        value_full = acc_v[...]
-        dk_ref[:, cols(h)] = key_full.astype(BF16)
-        dv_ref[:, cols(h)] = value_full.astype(BF16)
-        sq_all[z, 1, h] = jnp.sum(key_full * key_full, axis=0, keepdims=True)
-        sq_all[z, 2, h] = jnp.sum(value_full * value_full, axis=0, keepdims=True)
+            d = lax.rem(z + i, n)
+            skip = (d == guest) & is_host
+
+            @pl.when((h >= gc) | (inner(z) & jnp.logical_not(skip)))
+            def _():
+                eps_arrival(d, h).wait_recv()
+
+        for b in range(n):
+            part[b, h] = jnp.zeros((HD, rows), BF16)
+
+        @pl.loop(0, holders(h))
+        def _(k):
+            v = h + k * heads
+            acc_k[...] = jnp.zeros_like(acc_k)
+            acc_v[...] = jnp.zeros_like(acc_v)
+
+            @pl.loop(0, n)
+            def _(b):
+                logs = [lse_all[d, h, b] for d in range(n)]
+                top = functools.reduce(jnp.maximum, logs)
+                log_norm = top + jnp.log2(sum(jnp.exp2(x - top) for x in logs))
+                delta = sum(jnp.exp2(logs[d] - log_norm) * eps_all[d, h, b] for d in range(n))
+                share = jnp.exp2(top_ref[v, b] - log_norm)
+                q_b = q_all[b, :, cols(h)]
+                g_b = g_all[b, h]
+                dq_t = jnp.zeros((HD, rows), F32)
+                for j in range(key_tiles):
+                    at = slice(j * TILE, (j + 1) * TILE)
+                    p = probs[b, v, at, :].astype(F32) * share
+                    ds = (p * (dprobs(b, v, h, j) - delta)).astype(BF16)
+                    acc_v[at, :] += dot_nn(p.astype(BF16), g_b)
+                    acc_k[at, :] += dot_nn(ds, q_b)
+                    dq_t += dot_nn(kt_ref[v, :, at], ds)
+                part[b, h] = (part[b, h].astype(F32) + dq_t * scale).astype(BF16)
+
+            key_full = acc_k[...] * scale
+            value_full = acc_v[...]
+
+            @pl.when(k == 0)
+            def _():
+                dk_ref[:, cols(h)] = key_full.astype(BF16)
+                dv_ref[:, cols(h)] = value_full.astype(BF16)
+                sq_all[z, 1, h] = jnp.sum(key_full * key_full, axis=0, keepdims=True)
+                sq_all[z, 2, h] = jnp.sum(value_full * value_full, axis=0, keepdims=True)
+
+            if gc:
+                @pl.when(k == 1)
+                def _():
+                    guest_out[h, 0] = key_full.astype(BF16)
+                    guest_out[h, 1] = value_full.astype(BF16)
+                    back_copy(h).start()
+
+    def take_back(h):
+        @pl.when((h >= 0) & (h < gc) & is_end)
+        def _():
+            back_arrival(h).wait_recv()
+            for i, ref in enumerate((dk_ref, dv_ref)):
+                ref[:, cols(h)] = guest_in[h, i]
+                full = guest_in[h, i].astype(F32)
+                sq_all[z, i + 1, h] = jnp.sum(full * full, axis=0, keepdims=True)
+
+    def comes(h, way):
+        far = z if way == 0 else n - 1 - z
+        return far > jnp.where(h < gc, 1, 0)
+
+    def chain_sends(h, way, act):
+        for i in reversed(range(1, n)):
+            b = z + i if way == 0 else z - i
+
+            @pl.when((b >= 0) & (b < n) & ((h >= gc) | inner(z)))
+            def _():
+                act(b)
 
     def chain_hop(h, way):
-        first = has_left if way == 0 else has_right
+        def hop(b):
+            @pl.when(comes(h, way))
+            def _():
+                chain_arrival(b, h).wait_recv()
+                part[b, h] = (part[b, h].astype(F32) + chain[b, h].astype(F32)).astype(BF16)
+
+            chain_copy(b, h, way).start()
 
         @pl.when((h >= 0) & (h < heads))
         def _():
-            for i in range(1, n):
-                b = z + i if way == 0 else z - i
-
-                @pl.when((b >= 0) & (b < n))
-                def _():
-                    @pl.when(first)
-                    def _():
-                        chain_arrival(b, h).wait_recv()
-                        part[b, h] = (part[b, h].astype(F32) + chain[b, h].astype(F32)).astype(BF16)
-
-                    chain_copy(b, h, way).start()
+            chain_sends(h, way, hop)
 
     def own_sum(h):
         @pl.when((h >= 0) & (h < heads))
         def _():
-            acc_q[...] = part[z, h].astype(F32)
-
-            @pl.when(has_left)
-            def _():
-                chain_arrival(z, h).wait_recv()
-                acc_q[...] += chain[z, h].astype(F32)
-
-            @pl.when(has_right)
-            def _():
-                chain_arrival(n, h).wait_recv()
-                acc_q[...] += chain[n, h].astype(F32)
+            acc_q[...] = jnp.zeros_like(acc_q)
+
+            @pl.when((h >= gc) | inner(z))
+            def _():
+                acc_q[...] = part[z, h].astype(F32)
+
+            for way, slot in ((0, z), (1, n)):
+                @pl.when(comes(h, way))
+                def _():
+                    chain_arrival(slot, h).wait_recv()
+                    acc_q[...] += chain[slot, h].astype(F32)
 
             query_full = jnp.transpose(acc_q[...])
             dq_ref[:, cols(h)] = query_full.astype(BF16)
@@ -486,7 +607,14 @@
         @pl.when(t == 1)
         def _():
             for i in range(1, n):
-                lse_arrival(lax.rem(z + i, n)).wait_recv()
+                d = lax.rem(z + i, n)
+                lse_arrival(d, 0).wait_recv()
+                if gc:
+                    skip = (d == guest) & is_host
+
+                    @pl.when(inner(z) & jnp.logical_not(skip))
+                    def _():
+                        lse_arrival(d, 1).wait_recv()
 
         @pl.when((t >= 1) & (t <= heads))
         def _():
@@ -495,6 +623,8 @@
         chain_hop(t - 1 - z, 0)
         chain_hop(t - 1 - (n - 1 - z), 1)
         own_sum(t - 1 - jnp.maximum(z, n - 1 - z))
+        if gc:
+            take_back(t - 3)
 
     for i in range(1, n):
         sq_copy(i).start()
@@ -504,57 +634,51 @@
     mean = jnp.sum(total, axis=-1, keepdims=True) / (n * rows * HD)
     logs = jnp.log(mean + 1e-06)
     lane = lax.broadcasted_iota(jnp.int32, (1, HD), 1)
-    for h in range(heads):
-        feat_ref[h : h + 1, :] = sum(jnp.where(lane == j, logs[j, h], 0.0) for j in range(3))
+    for j in range(3):
+        feat_ref[j] = sum(jnp.where(lane == h, logs[j, h], 0.0) for h in range(heads))
 
     for i in range(1, nh):
         og_copy(i).wait_send()
     for i in range(1, n):
         sq_copy(i).wait_send()
-        lse_copy(i).wait_send()
-    both_ways(lambda way: q_own(way).wait_send())
+    lse_sends(lambda c: c.wait_send())
+    q_own_all(lambda c: c.wait_send())
     for s in range(1, n - 1):
-        @pl.when((z - s >= 0) & has_right)
-        def _():
-            q_copy(z - s, 0).wait_send()
-
-        @pl.when((z + s < n) & has_left)
-        def _():
-            q_copy(z + s, 1).wait_send()
+        q_on(s, lambda c: c.wait_send())
+    if gc:
+        @pl.when(is_end)
+        def _():
+            lend(0).wait_send()
+            lend(1).wait_send()
 
     @pl.loop(0, heads)
     def _(h):
-        both_ways(lambda way: g_copy(z, h, way).wait_send())
-        for s in range(1, n - 1):
-            @pl.when((z - s >= 0) & has_right)
-            def _():
-                g_copy(z - s, h, 0).wait_send()
-
-            @pl.when((z + s < n) & has_left)
-            def _():
-                g_copy(z + s, h, 1).wait_send()
-        for i in range(1, n):
-            eps_copy(h, i).wait_send()
-
-            @pl.when(z + i < n)
-            def _():
-                chain_copy(z + i, h, 0).wait_send()
-
-            @pl.when(z - i >= 0)
-            def _():
-                chain_copy(z - i, h, 1).wait_send()
+        for way in range(2):
+            for s in range(n - 1):
+                b = z - s if way == 0 else z + s
+
+                @pl.when((h >= gc) | inner(z) | (b == z))
+                def _():
+                    g_sends(b, h, way, lambda c: c.wait_send())
+
+            chain_sends(h, way, lambda b: chain_copy(b, h, way).wait_send())
+        eps_sends(h, lambda c: c.wait_send())
+        if gc:
+            @pl.when((h < gc) & is_host)
+            def _():
+                back_copy(h).wait_send()
 
 
 def finish_kernel(dq_in, dk_in, dv_in, feat_in, dq_ref, dk_ref, dv_ref, feat_ref):
     dq_ref[...] = dq_in[...]
     dk_ref[...] = dk_in[...]
     dv_ref[...] = dv_in[...]
-    feat_ref[...] = feat_in[:, : feat_ref.shape[1]]
+    feat_ref[...] = feat_in[:, :, : feat_ref.shape[2]]
 
 
 def fused_bytes(n, nh, rows, width, feats):
     block = rows * width * 2
-    kept = n * (width // HD) * rows * rows * 2
+    kept = n * (width // HD) * rows * rows * 3
     return block * (5 + 3 * n + n + 1) + rows * feats * 2 * nh + width * feats * nh * 2 + 2 * block + kept
 
 
@@ -570,41 +694,46 @@
     heads = width // HD
     key_tiles = rows // TILE
     wide = 256 if width % 256 == 0 else HD
+    gc = heads // 3 if n >= 4 else 0
+    gn = max(gc, 1)
     vmem = pl.BlockSpec(memory_space=pltpu.VMEM)
     dma = pltpu.SemaphoreType.DMA
     block = jax.ShapeDtypeStruct((rows, width), BF16)
     dq, dk, dv, feat = pl.pallas_call(
-        functools.partial(fused_kernel, n, nh),
-        out_shape=[block, block, block, jax.ShapeDtypeStruct((heads, HD), F32)],
+        functools.partial(fused_kernel, n, nh, gc),
+        out_shape=[block, block, block, jax.ShapeDtypeStruct((3, 1, HD), F32)],
         in_specs=[pl.BlockSpec(memory_space=pltpu.SMEM)] * 2 + [pl.BlockSpec(memory_space=pl.ANY)] * 5,
         out_specs=[vmem] * 4,
         scratch_shapes=[
-            pltpu.VMEM((rows, width), BF16),
-            pltpu.VMEM((rows, width), BF16),
+            pltpu.VMEM((rows, width + gc * HD), BF16),
+            pltpu.VMEM((rows, width + gc * HD), BF16),
             pltpu.VMEM((width, feats * nh), BF16),
-            pltpu.VMEM((n, key_tiles, 1, rows), F32),
+            pltpu.VMEM((2, n, key_tiles, 1, rows), F32),
             pltpu.VMEM((n, rows, width), BF16),
             pltpu.VMEM((n, heads, rows, HD), BF16),
             pltpu.VMEM((nh, rows, feats), BF16),
             pltpu.VMEM((width // wide, rows, wide), F32),
-            pltpu.VMEM((n, heads, rows, rows), BF16),
-            pltpu.VMEM((heads, n, 1, rows), F32),
-            pltpu.VMEM((heads, n, 1, rows), F32),
+            pltpu.VMEM((n, heads + gc, rows, rows), BF16),
+            pltpu.VMEM((heads + gc, n, 1, rows), F32),
+            pltpu.VMEM((heads + gc, n, 1, rows), F32),
             pltpu.VMEM((n, heads, n, 1, rows), F32),
             pltpu.VMEM((n, heads, n, 1, rows), F32),
             pltpu.VMEM((n, heads, HD, rows), BF16),
             pltpu.VMEM((n + 1, heads, HD, rows), BF16),
-            pltpu.VMEM((heads, HD, rows), BF16),
+            pltpu.VMEM((heads + gc, HD, rows), BF16),
             pltpu.VMEM((rows, HD), F32),
             pltpu.VMEM((rows, HD), F32),
             pltpu.VMEM((HD, rows), F32),
             pltpu.VMEM((n, 3, heads, 1, HD), F32),
+            pltpu.VMEM((gn, 2, rows, HD), BF16),
+            pltpu.VMEM((gn, 2, rows, HD), BF16),
+            dma((2,)), dma((2,)), dma((gn,)), dma((gn,)),
             dma((5,)),
             dma((nh,)), dma((nh,)),
-            dma((2, n)), dma((n,)),
+            dma((2, n, 2)), dma((n, 2)),
             dma((2, n, heads)), dma((n, heads)),
-            dma((n,)), dma((n,)),
-            dma((heads, n)), dma((n, heads)),
+            dma((n, 3)), dma((n, 2)),
+            dma((heads, n, 2)), dma((n, heads)),
             dma((n, heads)), dma((n + 1, heads)),
             dma((n,)), dma((n,)),
         ],
@@ -619,11 +748,11 @@
     )(key_list[0], key_count, query_states[0], key_states[0], value_states[0], output_grad[0], w_out)
     dq, dk, dv, grad_features = pl.pallas_call(
         finish_kernel,
-        out_shape=[block, block, block, jax.ShapeDtypeStruct((heads, 3), F32)],
+        out_shape=[block, block, block, jax.ShapeDtypeStruct((3, 1, heads), F32)],
         in_specs=[vmem] * 4,
         out_specs=[vmem] * 4,
     )(dq, dk, dv, feat)
-    return dq[None], dk[None], dv[None], grad_features[None]
+    return dq[None], dk[None], dv[None], jnp.transpose(grad_features, (1, 2, 0))
 
 
 def solution(mesh):

time: 171 us -> 152 us (0.89)
  Pallas kernels: 169 us -> 151 us
    pallas_call x1, Pallas kernels: 166 us -> 148 us  [per_device(): pl.pallas_call(functools.partial(fused_kernel, n, nh, gc), out_shape=[blo...]
where the time goes in v3:
time: 152 us
  Pallas kernels  151 us (99%)
    pallas_call x1, Pallas kernels, per_device(): pl.pallas_call(functools.partial(fused_kernel, n, nh, gc), out_shape=[blo...  148 us
    pallas_call x1, Pallas kernels, per_device(): pl.pallas_call(finish_kernel, out_shape=[block, block, block, jax.ShapeDt...  3.06 us

profile of v3, /device:TPU:0, one launch (start us, length us, event | category | flops | bytes accessed | tf_op | source)
XLA Modules:
  0.0 151.8 jit_solution(15806055283918511837)
XLA Ops:
  0.6 148.1 %shard_map.102 = (bf16[512,768]{1,0:T(8,128)(2,1)}, bf16[512,768]{1,0:T(8,128)(2,1)}, bf16[512,768]{1,0:T(8,128)(2,1)}, f32[3,1,128]{2,1,0:T(1,128)}) custom-call(s32[8,8]{1,0:T(8,128)} %bitcast.16, s32[1,8]{1,0:T(1,128)} %count_ref.1, bf16[512,768]{1,0:T(8,128)(2,1)} %bitcast.10, bf16[512,768]{1,0:T(8,128)(2,1)} %bitcast.11, bf16[512,768]{1,0:T(8,128)(2,1)} %bitcast.12, ...), custom_call_target="tpu_custom_call" | custom-call | flops 13690208256 | bytes 6291456 | tf_op jit(solution)/shard_map/pallas_call | solution.py:702
  148.7 3.1 %shard_map.103 = (bf16[512,768]{1,0:T(8,128)(2,1)}, bf16[512,768]{1,0:T(8,128)(2,1)}, bf16[512,768]{1,0:T(8,128)(2,1)}, f32[3,1,6]{2,1,0:T(1,128)}) custom-call(bf16[512,768]{1,0:T(8,128)(2,1)} %get-tuple-element.12.dq_in, bf16[512,768]{1,0:T(8,128)(2,1)} %get-tuple-element.13.dk_in, bf16[512,768]{1,0:T(8,128)(2,1)} %get-tuple-element.14.dv_in, ...), custom_call_target="tpu_custom_call" | custom-call | tf_op jit(solution)/shard_map/pallas_call | solution.py:749

commit v4 on v3

--- a/solution.py
+++ b/solution.py
@@ -164,6 +164,7 @@
 MESH_ID = pl.DeviceIdType.MESH
 VMEM_BYTES = 58 * 1024 * 1024
 NEG_BIG = -1e30
+OG_CUTS = 2
 F32 = jnp.float32
 BF16 = jnp.bfloat16
 
@@ -233,11 +234,15 @@
         pl.semaphore_signal(barrier, inc=1, device_id={"head": lax.rem(hx + i, nh)}, device_id_type=MESH_ID)
     pl.semaphore_wait(barrier, n - 1 + nh - 1)
 
-    def og_copy(i):
-        return remote(og_ref, og_all.at[hx], og_send.at[i], og_recv.at[hx], "head", lax.rem(hx + i, nh))
-
-    def og_arrival(j):
-        return remote(og_all.at[j], og_all.at[j], og_send.at[0], og_recv.at[j], "head", hx)
+    def og_rows(c):
+        return pl.ds(c * (rows // OG_CUTS), rows // OG_CUTS)
+
+    def og_copy(i, c):
+        return remote(og_ref.at[og_rows(c)], og_all.at[hx, og_rows(c)], og_send.at[i, c], og_recv.at[hx, c], "head", lax.rem(hx + i, nh))
+
+    def og_arrival(j, c):
+        ref = og_all.at[j, og_rows(c)]
+        return remote(ref, ref, og_send.at[0, c], og_recv.at[j, c], "head", hx)
 
     q_parts = [(0, gw), (gw, width - gw)] if gc else [(0, width)]
 
@@ -265,6 +270,10 @@
 
     def g_copy(b, h, way):
         return remote(g_all.at[b, h], g_all.at[b, h], g_send.at[way, b, h], g_recv.at[b, h], "seq", z + (1 - 2 * way))
+
+    def g_own(h, way, c):
+        ref = g_all.at[z, h, og_rows(c)]
+        return remote(ref, ref, g_send.at[way, z, h], g_recv.at[z, h], "seq", z + (1 - 2 * way))
 
     def lse_ref(d, p):
         return lse_all.at[d, 0:gc] if p else lse_all.at[d, gc:heads]
@@ -330,13 +339,20 @@
                 def _():
                     act(q_copy(b, way, p))
 
+    def g_own_starts(h, c):
+        for way in range(2):
+            @pl.when(may_go(way, False) & ((h >= gc) | may_go(way, True)))
+            def _():
+                g_own(h, way, c).start()
+
     def g_sends(b, h, way, act):
         @pl.when((b >= 0) & (b < n) & may_go(way, False) & ((h >= gc) | may_go(way, True)))
         def _():
             act(g_copy(b, h, way))
 
     for i in range(1, nh):
-        og_copy(i).start()
+        for c in range(OG_CUTS):
+            og_copy(i, c).start()
     q_own_all(lambda c: c.start())
     if gc:
         @pl.when(is_end)
@@ -357,21 +373,32 @@
 
     wide = 256 if width % 256 == 0 else HD
 
-    def features_of(block, j, add):
+    def features_of(block, j, part_rows, add):
         span = pl.ds(pl.multiple_of(j * feats, HD), feats)
 
         @pl.loop(0, width // wide)
         def _(c):
             at = pl.ds(pl.multiple_of(c * wide, wide), wide)
-            term = dot_nt(block[...], w_ref[at, span])
+            term = dot_nt(block[part_rows, :], w_ref[at, span])
             if add:
-                g_acc[c] = g_acc[c] + term
+                g_acc[c, part_rows, :] = g_acc[c, part_rows, :] + term
             else:
-                g_acc[c] = term
+                g_acc[c, part_rows, :] = term
 
     for load in loads:
         load.wait()
-    features_of(og_all.at[hx], hx, False)
+    features_of(og_all.at[hx], hx, slice(0, rows), False)
+
+    def gradient_rows(c):
+        part_rows = og_rows(c)
+        for i in range(1, nh):
+            j = lax.rem(hx + i, nh)
+            og_arrival(j, c).wait_recv()
+            features_of(og_all.at[j], j, part_rows, True)
+        for h in range(heads):
+            lo = h * HD
+            g_all[z, h, part_rows, :] = g_acc[lo // wide, part_rows, lo % wide : lo % wide + HD].astype(BF16)
+            g_own_starts(h, c)
 
     def q_hop(s):
         for way, b in ((0, z - s), (1, z + s)):
@@ -421,24 +448,13 @@
         kt_ref[h] = jnp.transpose(k_ref[:, cols(h)].astype(F32)).astype(BF16)
 
     softmax_rows(z, first_head, heads)
-    early = min(2, n - 1)
-    for s in range(1, early + 1):
-        q_hop(s)
-        if s < early:
+    for s in range(1, max(n, OG_CUTS + 1)):
+        if s < n:
+            q_hop(s)
+        if s <= OG_CUTS:
+            gradient_rows(s - 1)
+        if s < n:
             softmax_at(s)
-    for i in range(1, nh):
-        j = lax.rem(hx + i, nh)
-        og_arrival(j).wait_recv()
-        features_of(og_all.at[j], j, True)
-    for h in range(heads):
-        lo = h * HD
-        g_all[z, h] = g_acc[lo // wide, :, lo % wide : lo % wide + HD].astype(BF16)
-        for way in range(2):
-            g_sends(z, h, way, lambda c: c.start())
-    softmax_at(early)
-    for s in range(early + 1, n):
-        q_hop(s)
-        softmax_at(s)
     if gc:
         @pl.when(is_host)
         def _():
@@ -638,7 +654,8 @@
         feat_ref[j] = sum(jnp.where(lane == h, logs[j, h], 0.0) for h in range(heads))
 
     for i in range(1, nh):
-        og_copy(i).wait_send()
+        for c in range(OG_CUTS):
+            og_copy(i, c).wait_send()
     for i in range(1, n):
         sq_copy(i).wait_send()
     lse_sends(lambda c: c.wait_send())
@@ -729,7 +746,7 @@
             pltpu.VMEM((gn, 2, rows, HD), BF16),
             dma((2,)), dma((2,)), dma((gn,)), dma((gn,)),
             dma((5,)),
-            dma((nh,)), dma((nh,)),
+            dma((nh, OG_CUTS)), dma((nh, OG_CUTS)),
             dma((2, n, 2)), dma((n, 2)),
             dma((2, n, heads)), dma((n, heads)),
             dma((n, 3)), dma((n, 2)),

time: 152 us -> 150 us (0.987)
  Pallas kernels: 151 us -> 149 us
    pallas_call x1, Pallas kernels: 148 us -> 146 us  [per_device(): pl.pallas_call(functools.partial(fused_kernel, n, nh, gc), out_shape=[blo...]
where the time goes in v4:
time: 150 us
  Pallas kernels  149 us (99%)
    pallas_call x1, Pallas kernels, per_device(): pl.pallas_call(functools.partial(fused_kernel, n, nh, gc), out_shape=[blo...  146 us
    pallas_call x1, Pallas kernels, per_device(): pl.pallas_call(finish_kernel, out_shape=[block, block, block, jax.ShapeDt...  3.06 us

profile of v4, /device:TPU:0, one launch (start us, length us, event | category | flops | bytes accessed | tf_op | source)
XLA Modules:
  0.0 149.6 jit_solution(3058109786876826117)
XLA Ops:
  0.6 145.9 %shard_map.102 = (bf16[512,768]{1,0:T(8,128)(2,1)}, bf16[512,768]{1,0:T(8,128)(2,1)}, bf16[512,768]{1,0:T(8,128)(2,1)}, f32[3,1,128]{2,1,0:T(1,128)}) custom-call(s32[8,8]{1,0:T(8,128)} %bitcast.16, s32[1,8]{1,0:T(1,128)} %count_ref.1, bf16[512,768]{1,0:T(8,128)(2,1)} %bitcast.10, bf16[512,768]{1,0:T(8,128)(2,1)} %bitcast.11, bf16[512,768]{1,0:T(8,128)(2,1)} %bitcast.12, ...), custom_call_target="tpu_custom_call" | custom-call | flops 13690208256 | bytes 6291456 | tf_op jit(solution)/shard_map/pallas_call | solution.py:719
  146.6 3.1 %shard_map.103 = (bf16[512,768]{1,0:T(8,128)(2,1)}, bf16[512,768]{1,0:T(8,128)(2,1)}, bf16[512,768]{1,0:T(8,128)(2,1)}, f32[3,1,6]{2,1,0:T(1,128)}) custom-call(bf16[512,768]{1,0:T(8,128)(2,1)} %get-tuple-element.12.dq_in, bf16[512,768]{1,0:T(8,128)(2,1)} %get-tuple-element.13.dk_in, bf16[512,768]{1,0:T(8,128)(2,1)} %get-tuple-element.14.dv_in, ...), custom_call_target="tpu_custom_call" | custom-call | tf_op jit(solution)/shard_map/pallas_call | solution.py:766

commit v5 on v4

--- a/solution.py
+++ b/solution.py
@@ -165,6 +165,7 @@
 VMEM_BYTES = 58 * 1024 * 1024
 NEG_BIG = -1e30
 OG_CUTS = 2
+AHEAD = 1
 F32 = jnp.float32
 BF16 = jnp.bfloat16
 
@@ -455,6 +456,24 @@
             gradient_rows(s - 1)
         if s < n:
             softmax_at(s)
+    def g_hop(s, h):
+        for way, b in ((0, z - s), (1, z + s)):
+            @pl.when((h >= 0) & (h < heads) & (b >= 0) & (b < n) & ((h >= gc) | inner(z)))
+            def _():
+                g_copy(b, h, way).wait_recv()
+                if s < n - 1:
+                    g_sends(b, h, way, lambda c: c.start())
+
+    def g_hops(t):
+        for s in range(1, n):
+            g_hop(s, t + (n - 1 - s) + AHEAD)
+
+    lead = n - 2 + AHEAD
+
+    @pl.loop(0, lead)
+    def _(step):
+        g_hops(step - lead)
+
     if gc:
         @pl.when(is_host)
         def _():
@@ -470,14 +489,6 @@
                 softmax_rows(b, heads, heads + gc)
 
     lse_sends(lambda c: c.start())
-
-    def g_hop(s, h):
-        for way, b in ((0, z - s), (1, z + s)):
-            @pl.when((h >= 0) & (h < heads) & (b >= 0) & (b < n) & ((h >= gc) | inner(z)))
-            def _():
-                g_copy(b, h, way).wait_recv()
-                if s < n - 1:
-                    g_sends(b, h, way, lambda c: c.start())
 
     def dprobs(b, v, h, j):
         return dot_nt(v_ref[j * TILE : (j + 1) * TILE, cols(v)], g_all[b, h])
@@ -608,13 +619,9 @@
             dq_ref[:, cols(h)] = query_full.astype(BF16)
             sq_all[z, 0, h] = jnp.sum(query_full * query_full, axis=0, keepdims=True)
 
-    lead = max(n - 2, 0)
-
-    @pl.loop(0, lead + heads + n)
-    def _(step):
-        t = step - lead
-        for s in range(1, n):
-            g_hop(s, t + (n - 1 - s))
+    @pl.loop(0, heads + n)
+    def _(t):
+        g_hops(t)
 
         @pl.when((t >= 0) & (t < heads))
         def _():
@@ -711,7 +718,7 @@
     heads = width // HD
     key_tiles = rows // TILE
     wide = 256 if width % 256 == 0 else HD
-    gc = heads // 3 if n >= 4 else 0
+    gc = 2 * heads // 3 if n >= 4 else 0
     gn = max(gc, 1)
     vmem = pl.BlockSpec(memory_space=pltpu.VMEM)
     dma = pltpu.SemaphoreType.DMA

time: 150 us -> 153 us (1.020)
  Pallas kernels: 149 us -> 152 us
    pallas_call x1, Pallas kernels: 146 us -> 149 us  [per_device(): pl.pallas_call(functools.partial(fused_kernel, n, nh, gc), out_shape=[blo...]
where the time goes in v5:
time: 153 us
  Pallas kernels  152 us (99%)
    pallas_call x1, Pallas kernels, per_device(): pl.pallas_call(functools.partial(fused_kernel, n, nh, gc), out_shape=[blo...  149 us
    pallas_call x1, Pallas kernels, per_device(): pl.pallas_call(finish_kernel, out_shape=[block, block, block, jax.ShapeDt...  3.06 us

profile of v5, /device:TPU:0, one launch (start us, length us, event | category | flops | bytes accessed | tf_op | source)
XLA Modules:
  0.0 152.5 jit_solution(11560636856691272636)
XLA Ops:
  0.6 148.8 %shard_map.102 = (bf16[512,768]{1,0:T(8,128)(2,1)}, bf16[512,768]{1,0:T(8,128)(2,1)}, bf16[512,768]{1,0:T(8,128)(2,1)}, f32[3,1,128]{2,1,0:T(1,128)}) custom-call(s32[8,8]{1,0:T(8,128)} %bitcast.16, s32[1,8]{1,0:T(1,128)} %count_ref.1, bf16[512,768]{1,0:T(8,128)(2,1)} %bitcast.10, bf16[512,768]{1,0:T(8,128)(2,1)} %bitcast.11, bf16[512,768]{1,0:T(8,128)(2,1)} %bitcast.12, ...), custom_call_target="tpu_custom_call" | custom-call | flops 13690208256 | bytes 6291456 | tf_op jit(solution)/shard_map/pallas_call | solution.py:726
  149.5 3.1 %shard_map.103 = (bf16[512,768]{1,0:T(8,128)(2,1)}, bf16[512,768]{1,0:T(8,128)(2,1)}, bf16[512,768]{1,0:T(8,128)(2,1)}, f32[3,1,6]{2,1,0:T(1,128)}) custom-call(bf16[512,768]{1,0:T(8,128)(2,1)} %get-tuple-element.12.dq_in, bf16[512,768]{1,0:T(8,128)(2,1)} %get-tuple-element.13.dk_in, bf16[512,768]{1,0:T(8,128)(2,1)} %get-tuple-element.14.dv_in, ...), custom_call_target="tpu_custom_call" | custom-call | tf_op jit(solution)/shard_map/pallas_call | solution.py:773

commit v6 on v5

--- a/solution.py
+++ b/solution.py
@@ -600,6 +600,12 @@
         def _():
             chain_sends(h, way, hop)
 
+    def chain_hops(t, starts):
+        for way, far in ((0, z), (1, n - 1 - z)):
+            @pl.when((far == 0) if starts else (far > 0))
+            def _():
+                chain_hop(t - 1 - far, way)
+
     def own_sum(h):
         @pl.when((h >= 0) & (h < heads))
         def _():
@@ -627,6 +633,8 @@
         def _():
             first_pass(t)
 
+        chain_hops(t, False)
+
         @pl.when(t == 1)
         def _():
             for i in range(1, n):
@@ -643,8 +651,7 @@
         def _():
             second_pass(t - 1)
 
-        chain_hop(t - 1 - z, 0)
-        chain_hop(t - 1 - (n - 1 - z), 1)
+        chain_hops(t, True)
         own_sum(t - 1 - jnp.maximum(z, n - 1 - z))
         if gc:
             take_back(t - 3)
@@ -718,7 +725,7 @@
     heads = width // HD
     key_tiles = rows // TILE
     wide = 256 if width % 256 == 0 else HD
-    gc = 2 * heads // 3 if n >= 4 else 0
+    gc = heads // 3 if n >= 4 else 0
     gn = max(gc, 1)
     vmem = pl.BlockSpec(memory_space=pltpu.VMEM)
     dma = pltpu.SemaphoreType.DMA

time: 153 us -> 152 us (level)
  no operation moved by 1% of the time
where the time goes in v6:
time: 152 us
  Pallas kernels  152 us (100%)
    pallas_call x1, Pallas kernels, per_device(): pl.pallas_call(functools.partial(fused_kernel, n, nh, gc), out_shape=[blo...  149 us
    pallas_call x1, Pallas kernels, per_device(): pl.pallas_call(finish_kernel, out_shape=[block, block, block, jax.ShapeDt...  3.06 us

profile of v6, /device:TPU:0, one launch (start us, length us, event | category | flops | bytes accessed | tf_op | source)
XLA Modules:
  0.0 152.2 jit_solution(7009526158007719541)
XLA Ops:
  0.6 148.5 %shard_map.102 = (bf16[512,768]{1,0:T(8,128)(2,1)}, bf16[512,768]{1,0:T(8,128)(2,1)}, bf16[512,768]{1,0:T(8,128)(2,1)}, f32[3,1,128]{2,1,0:T(1,128)}) custom-call(s32[8,8]{1,0:T(8,128)} %bitcast.16, s32[1,8]{1,0:T(1,128)} %count_ref.1, bf16[512,768]{1,0:T(8,128)(2,1)} %bitcast.10, bf16[512,768]{1,0:T(8,128)(2,1)} %bitcast.11, bf16[512,768]{1,0:T(8,128)(2,1)} %bitcast.12, ...), custom_call_target="tpu_custom_call" | custom-call | flops 13690208256 | bytes 6291456 | tf_op jit(solution)/shard_map/pallas_call | solution.py:733
  149.2 3.1 %shard_map.103 = (bf16[512,768]{1,0:T(8,128)(2,1)}, bf16[512,768]{1,0:T(8,128)(2,1)}, bf16[512,768]{1,0:T(8,128)(2,1)}, f32[3,1,6]{2,1,0:T(1,128)}) custom-call(bf16[512,768]{1,0:T(8,128)(2,1)} %get-tuple-element.12.dq_in, bf16[512,768]{1,0:T(8,128)(2,1)} %get-tuple-element.13.dk_in, bf16[512,768]{1,0:T(8,128)(2,1)} %get-tuple-element.14.dv_in, ...), custom_call_target="tpu_custom_call" | custom-call | tf_op jit(solution)/shard_map/pallas_call | solution.py:780
